TPU v7x, 256 devices: a whole 4x4x8 slice. The times are simulated.
256 devices in a mesh: gx: 16 (over z, core), gy: 16 (over y, x).
Axes of the slice: x: 4, y: 4, z: 8, core: 2. Of those that a mesh axis runs over, the one named last changes fastest.
Arguments:
- initial: float32 [2048, 4096], P(('gx', 'gy')), may hold values from -3 to 3
- source: float32 [2048, 4096], P(('gx', 'gy')), may hold values from -6 to 6
- permeability: float32 [2048, 4096], P(('gx', 'gy')), may hold values from 0.5 to 4
- migrate_x: int32 [2048], P(('gx', 'gy')), may hold values from 0 to 15, as said below
- migrate_y: int32 [2048], P(('gx', 'gy')), may hold values from 0 to 15, as said below
- neighbours: int32 [2048, 6], P(('gx', 'gy')), may hold values from -1 to 39, as said below
- children: int32 [2048], P(('gx', 'gy')), may hold values from 0 to 23, as said below
- parents: int32 [2048], P(('gx', 'gy')), may hold values from 0 to 23, as said below
Outputs:
- solution: float32 [2048, 4096], P(('gx', 'gy'))
- residual: float32 [2048, 4096], P(('gx', 'gy'))
Inputs may be any that keep to these rules, and one draw needn't show every extreme that they name: `migrate_x`: within each pair of devices whose gx index differs in the lowest bit, every block of the pair lands in exactly one slot; a device takes at most 2 blocks from its partner, and some device takes exactly 2. `migrate_y`: refers to the layout after the gx migration; within each pair of devices whose gy index differs in the lowest bit, every block lands in exactly one slot; a device takes at most 2 blocks from its partner, and some device takes exactly 2. `neighbours`: refers to the layout after both migrations; never names a device outside the mesh; on each device at most 6 entries name one given neighbouring device, and exactly 6 wherever that device exists. `children`: refers to the layout after both migrations; every block of every device is named by exactly one position; on each device exactly 1 entries name the gx partner and exactly 1 the gy partner. `parents`: the inverse of children: the position whose entry names the block, as src * 8 + position with src 0 own device, 1 the gx partner, 2 the gy partner; on each device exactly 1 entries have src 1 and exactly 1 src 2.
All inputs are finite; a program needn't handle non-finite values.
Results may differ from a plain program's by a relative error of at most 0.00002.
Values sent between devices are 32-bit elements; how exact they have to be, the bound alone decides.
A program may use at most 192 MiB of HBM per device.

v0:
```python
import functools

import jax
import jax.numpy as jnp
from jax import lax
from jax.experimental import pallas as pl
from jax.experimental.pallas import tpu as pltpu
from jax.sharding import PartitionSpec as P

INNER = 3
COARSE = 4
REACTION = 0.25
DAMPING = 0.8
OPP = (1, 0, 3, 2)

F32 = jnp.float32
I32 = jnp.int32
BF16 = jnp.bfloat16

_ROWS = lax.GatherDimensionNumbers(
    offset_dims=(),
    collapsed_slice_dims=(0,),
    start_index_map=(0,),
    operand_batching_dims=(1,),
    start_indices_batching_dims=(1,),
)


def rows(x, index):
    return lax.gather(
        x, index[..., None], _ROWS, (1, 1), mode=lax.GatherScatterMode.PROMISE_IN_BOUNDS
    )


def roll(x, shift):
    return pltpu.roll(x, shift % 128, 1) if shift % 128 else x


def split3(x):
    high = x.astype(BF16)
    rest = x - high.astype(F32)
    mid = rest.astype(BF16)
    low = (rest - mid.astype(F32)).astype(BF16)
    return high, mid, low


def exact_dot(x, matrix):
    count = x.shape[0]
    out = jnp.dot(jnp.concatenate(split3(x), 0), matrix, preferred_element_type=F32)
    return out[:count] + (out[count : 2 * count] + out[2 * count :])


def kernel(
    init_h, src_h, perm_h, mx_h, my_h, nb_h, ch_h, pa_h, sol_h, res_h,
    own, px, t_mx, t_my, t_ch, t_pa, nbv, msg_s, msg_r, yi_s, yi_r, yf_s, yf_r,
    va, vb, fr, qr, sb, sc, gb, gc, gs, gr, ps, pxr, pyr, pd_s, pd_r,
    ea, eb, e0, ef, eq, cor, zz, restrict_m, upsample_m, sol_v, res_v,
    lsem, ssem, rsem,
):
    i, j = lax.axis_index("gx"), lax.axis_index("gy")
    nx, ny = lax.axis_size("gx"), lax.axis_size("gy")
    xp = (i + 1 - 2 * (i % 2), j)
    yp = (i, j + 1 - 2 * (j % 2))
    diag = (xp[0], yp[1])
    around = (((i + nx - 1) % nx, j), ((i + 1) % nx, j), (i, (j + ny - 1) % ny), (i, (j + 1) % ny))

    barrier = pltpu.get_barrier_semaphore()
    for peer in around + (diag,):
        pl.semaphore_signal(barrier, inc=1, device_id=peer, device_id_type=pl.DeviceIdType.MESH)

    tables = [
        pltpu.make_async_copy(a, b, lsem.at[n])
        for n, (a, b) in enumerate(
            ((mx_h, t_mx), (my_h, t_my), (ch_h, t_ch), (pa_h, t_pa), (nb_h, nbv))
        )
    ]
    for copy in tables:
        copy.start()
    fields = [
        pltpu.make_async_copy(a, own.at[n], lsem.at[5 + n])
        for n, a in enumerate((init_h, src_h, perm_h))
    ]
    for copy in fields:
        copy.start()

    used = [0]

    def push(source, target, peer, there=None):
        n = used[0]
        if there is None:
            there = n
            used[0] += 1
        return pltpu.make_async_remote_copy(
            src_ref=source,
            dst_ref=target,
            send_sem=ssem.at[n if there == n else n],
            recv_sem=rsem.at[there],
            device_id=peer,
            device_id_type=pl.DeviceIdType.MESH,
        )

    def push_around(sources, target):
        base = used[0]
        used[0] += 4
        return [
            pltpu.make_async_remote_copy(
                src_ref=sources(d),
                dst_ref=target(OPP[d]),
                send_sem=ssem.at[base + d],
                recv_sem=rsem.at[base + OPP[d]],
                device_id=around[d],
                device_id_type=pl.DeviceIdType.MESH,
            )
            for d in range(4)
        ]

    pl.semaphore_wait(barrier, 5)
    x_copies = [push(a, px.at[n], xp) for n, a in enumerate((init_h, src_h, perm_h))]
    for copy in x_copies:
        copy.start()

    lane = lax.broadcasted_iota(I32, (8, 128), 1)
    sub = lax.broadcasted_iota(I32, (8, 128), 0)
    zero = jnp.zeros((8, 128), F32)

    for copy in tables:
        copy.wait()

    def column(ref):
        out = jnp.full((8, 128), ref[0], I32)
        for k in range(1, 8):
            out = jnp.where(sub == k, ref[k], out)
        return out

    mx, my, ch, pa = column(t_mx), column(t_my), column(t_ch), column(t_pa)

    links = [jnp.broadcast_to(nbv[:, f : f + 1], (8, 128)) for f in range(6)]
    away = [jnp.where(c >= 0, c // 8, 7) for c in links]
    slot = [jnp.where(c >= 0, c % 8, 0) for c in links]
    marks = jnp.concatenate([(lane == d).astype(F32) for d in away], 0)
    before = (
        lax.broadcasted_iota(I32, (48, 48), 1) < lax.broadcasted_iota(I32, (48, 48), 0)
    ).astype(F32)
    counts = jnp.dot(before, marks, preferred_element_type=F32)
    rank = []
    wanted = zero
    for f in range(6):
        mine = jnp.where(lane == away[f], counts[8 * f : 8 * f + 8], 0.0)
        place = jnp.broadcast_to(jnp.sum(mine, axis=1, keepdims=True), (8, 128)).astype(I32)
        place = jnp.minimum(place, 7)
        rank.append(place)
        remote = (away[f] >= 1) & (away[f] <= 4)
        hit = (lane == away[f] * 8 + place) & remote
        wanted = wanted + jnp.where(hit, ((f ^ 1) * 8 + slot[f]).astype(F32), 0.0)
    msg_s[0:8, :] = jnp.broadcast_to(jnp.sum(wanted, axis=0, keepdims=True), (8, 128))
    msg_s[8:16, :] = ch.astype(F32)
    msgs = push_around(lambda d: msg_s, lambda d: msg_r.at[d])
    for copy in msgs:
        copy.start()

    named = sub == t_my[0]
    for k in range(1, 8):
        named = named | (sub == t_my[k])
    free = jnp.where(named, 8.0, sub.astype(F32))
    first = jnp.min(free, axis=0, keepdims=True)
    last = jnp.max(jnp.where(named, 0.0, sub.astype(F32)), axis=0, keepdims=True)
    leave = jnp.where(sub % 2 == 0, jnp.broadcast_to(first, (8, 128)), jnp.broadcast_to(last, (8, 128)))
    leave = jnp.minimum(leave, 7.0).astype(I32)
    leave_e = rows(mx, leave)
    leave_own, leave_row = leave_e < 8, leave_e % 8
    stay = my < 8
    final_e = rows(mx, my % 8)
    final_own, final_row = final_e < 8, final_e % 8
    order = jnp.zeros((8, 128), I32)
    for k in range(8):
        entry = t_my[k]
        order = order + jnp.where((entry >= 8) & (my > entry), 1, 0)
    final_first = order == 0

    fine = lax.broadcasted_iota(I32, (256, 128), 0)
    small = lax.broadcasted_iota(I32, (256, 128), 1)
    same = (fine // 32 == small // 16) & ((fine % 16) // 2 == small % 8)
    restrict_m[...] = jnp.where(same, 0.125, 0.0).astype(BF16)
    fine = lax.broadcasted_iota(I32, (128, 256), 1)
    small = lax.broadcasted_iota(I32, (128, 256), 0)
    same = (fine // 32 == small // 16) & ((fine % 16) // 2 == small % 16)
    upsample_m[...] = jnp.where(same, 1.0, 0.0).astype(BF16)

    def leaving(n, c):
        cols = pl.ds(128 * c, 128)
        return jnp.where(leave_own, rows(own[n, :, cols], leave_row), rows(px[n, :, cols], leave_row))

    fields[0].wait()
    x_copies[0].wait_recv()
    for c in range(32):
        yi_s[c] = leaving(0, c)[0:2]
    y_first = push(yi_s, yi_r, yp)
    y_first.start()
    for n in (1, 2):
        fields[n].wait()
        x_copies[n].wait_recv()
    for c in range(32):
        yf_s[c] = jnp.where(sub < 2, leaving(1, c), leaving(2, c))[0:4]
    y_second = push(yf_s, yf_r, yp)
    y_second.start()

    for copy in msgs:
        copy.wait_recv()
    give = []
    for d in range(4):
        code = jnp.where(lane == (OPP[d] + 1) * 8 + sub, msg_r[d, 0:8, :], 0.0)
        code = jnp.broadcast_to(jnp.sum(code, axis=1, keepdims=True), (8, 128)).astype(I32)
        give.append((code // 8, code % 8))
    ch_x = msg_r[1 - i % 2, 8:16, :].astype(I32)
    ch_y = msg_r[3 - j % 2, 8:16, :].astype(I32)

    def arrived(n, ref, top, c):
        cols = pl.ds(128 * c, 128)
        kept = jnp.where(final_own, rows(own[n, :, cols], final_row), rows(px[n, :, cols], final_row))
        one = jnp.broadcast_to(ref[c, top : top + 1, :], (8, 128))
        two = jnp.broadcast_to(ref[c, top + 1 : top + 2, :], (8, 128))
        return jnp.where(stay, kept, jnp.where(final_first, one, two))

    low_b, high_b = lane < 16, lane >= 112
    low_c, high_c = lane % 16 == 0, lane % 16 == 15
    left_half, left_c = lane < 64, lane % 16 < 8
    group, inside = lane // 16, lane % 16
    row_b = jnp.where(left_half, slot[2], slot[3])
    here_b = jnp.where(left_half, away[2], away[3]) == 0
    row_c = jnp.where(left_c, slot[4], slot[5])
    here_c = jnp.where(left_c, away[4], away[5]) == 0

    def send_faces(g, v):
        packed = [[v[1, :, 0:128], v[1, :, 128:256]], [v[16, :, 0:128], v[16, :, 128:256]]]
        for _ in range(4):
            packed.append([zero, zero])
        for a in range(16):
            both = jnp.where(left_half, roll(v[a + 1, :, 128:256], 16), roll(v[a + 1, :, 0:128], -16))
            sb[a] = both
            moved = roll(both, 16 * (a % 8))
            packed[3][a // 8] = jnp.where(group == a % 8, moved, packed[3][a // 8])
            packed[2][a // 8] = jnp.where(group == (a + 7) % 8, moved, packed[2][a // 8])
            for h in range(2):
                half = v[a + 1, :, 128 * h : 128 * h + 128]
                both = jnp.where(left_c, roll(half, -15), roll(half, 15))
                sc[a, :, 128 * h : 128 * h + 128] = both
                m, k = (2 * a + h) % 16, (2 * a + h) // 16
                moved = roll(both, m)
                packed[5][k] = jnp.where(inside == m, moved, packed[5][k])
                packed[4][k] = jnp.where(inside == (m + 15) % 16, moved, packed[4][k])
        for d in range(4):
            face, row = give[d]
            for k in range(2):
                out = rows(packed[0][k], row)
                for f in range(1, 6):
                    out = jnp.where(face == f, rows(packed[f][k], row), out)
                gs[g, d, :, 128 * k : 128 * k + 128] = out
        copies = push_around(lambda d: gs.at[g, d], lambda d: gr.at[g, d])
        for copy in copies:
            copy.start()
        return copies

    def take_faces(g, v, ends, copies):
        for copy in copies:
            copy.wait_recv()
        came = [[zero, zero] for _ in range(6)]
        for f in range(6):
            for k in range(2):
                for d in range(4):
                    got = rows(gr[g, d, :, 128 * k : 128 * k + 128], rank[f])
                    came[f][k] = jnp.where(away[f] == d + 1, got, came[f][k])
        for k in range(2):
            cols = slice(128 * k, 128 * k + 128)
            low = jnp.where(away[0] == 0, rows(v[16, :, cols], slot[0]), came[0][k])
            high = jnp.where(away[1] == 0, rows(v[1, :, cols], slot[1]), came[1][k])
            for end in ends:
                end[0, :, cols] = low
                end[17, :, cols] = high
        for a in range(16):
            both = jnp.where(group == a % 8, came[2][a // 8], came[3][a // 8])
            gb[a] = jnp.where(here_b, rows(sb[a], row_b), roll(both, -16 * (a % 8)))
            for h in range(2):
                cols = slice(128 * h, 128 * h + 128)
                m, k = (2 * a + h) % 16, (2 * a + h) // 16
                both = jnp.where(inside == m, came[4][k], came[5][k])
                gc[a, :, cols] = jnp.where(here_c, rows(sc[a, :, cols], row_c), roll(both, -m))

    def stencil(v, a, ghost_b, ghost_c):
        x = [v[a + 1, :, 0:128], v[a + 1, :, 128:256]]
        down, up = [roll(y, 16) for y in x], [roll(y, -16) for y in x]
        beside_b = (
            (jnp.where(low_b, ghost_b, down[0]), jnp.where(high_b, up[1], up[0])),
            (jnp.where(low_b, down[0], down[1]), jnp.where(high_b, ghost_b, up[1])),
        )
        out = []
        for h in range(2):
            cols = slice(128 * h, 128 * h + 128)
            beside = beside_b[h] + (
                jnp.where(low_c, ghost_c[h], roll(x[h], 1)),
                jnp.where(high_c, ghost_c[h], roll(x[h], -1)),
                v[a, :, cols],
                v[a + 2, :, cols],
            )
            mobility = 1.0 + x[h] * x[h]
            squares, flux = 6.0 * mobility, None
            for w in beside:
                square = w * w
                squares = squares + square
                term = (mobility + square) * (x[h] - w)
                flux = term if flux is None else flux + term
            out.append((x[h], flux, squares))
        return out

    def fine_ghosts(a):
        return gb[a], (gc[a, :, 0:128], gc[a, :, 128:256])

    def over(count, step):
        lax.fori_loop(0, count, lambda a, carry: (step(a), carry)[1], 0, unroll=4)

    def jacobi(v, force, coefficient, ghosts, store, count):
        def step(a):
            parts = stencil(v, a, *ghosts(a))
            for h, (x, flux, conduct) in enumerate(parts):
                cols = slice(128 * h, 128 * h + 128)
                q = coefficient[a, :, cols]
                defect = force[a, :, cols] - (REACTION * x + q * flux)
                store(a, h, x + DAMPING * defect / (REACTION + q * conduct))

        over(count, step)

    def into(ref):
        def store(a, h, value):
            ref[a + 1, :, 128 * h : 128 * h + 128] = value

        return store

    def shrink(n, layer):
        fold = jnp.concatenate([layer(2 * a) + layer(2 * a + 1) for a in range(8)], 0)
        out = exact_dot(fold, restrict_m[...])
        for a in range(8):
            zz[n, a] = out[8 * a : 8 * a + 8]
        for m in range(4):
            dense = jnp.where(left_c, out[16 * m : 16 * m + 8], out[16 * m + 8 : 16 * m + 16])
            ps[n, m] = dense
            pd_s[n, m] = rows(dense, outward)[0:2]
        copies = [
            push(ps.at[n], pxr.at[n], xp),
            push(ps.at[n], pyr.at[n], yp),
            push(pd_s.at[n], pd_r.at[n], diag),
        ]
        for copy in copies:
            copy.start()
        return copies

    slots = sub.astype(F32)
    to_x = jnp.sum(jnp.where(pa // 8 == 1, slots, 0.0), axis=0, keepdims=True)
    to_y = jnp.sum(jnp.where(pa // 8 == 2, slots, 0.0), axis=0, keepdims=True)
    outward = jnp.where(sub == 0, jnp.broadcast_to(to_x, (8, 128)), jnp.broadcast_to(to_y, (8, 128)))
    outward = outward.astype(I32)

    y_first.wait_recv()
    for c in range(32):
        va[1 + c // 2, :, 128 * (c % 2) : 128 * (c % 2) + 128] = arrived(0, yi_r, 0, c)
    copies0 = send_faces(0, va)
    y_second.wait_recv()
    for c in range(32):
        cols = slice(128 * (c % 2), 128 * (c % 2) + 128)
        fr[c // 2, :, cols] = arrived(1, yf_r, 0, c)
        qr[c // 2, :, cols] = 0.5 * arrived(2, yf_r, 2, c)
    perm_copies = shrink(2, lambda a: qr[a])
    take_faces(0, va, (va, vb), copies0)

    for source, target in ((va, vb), (vb, va), (va, vb)):
        jacobi(source, fr, qr, fine_ghosts, into(target), 16)

    copies1 = send_faces(1, vb)
    sol_copies = shrink(0, lambda a: vb[a + 1])
    take_faces(1, vb, (vb,), copies1)

    def residual_step(a):
        for h, (x, flux, _) in enumerate(stencil(vb, a, *fine_ghosts(a))):
            cols = slice(128 * h, 128 * h + 128)
            value = fr[a, :, cols] - (REACTION * x + qr[a, :, cols] * flux)
            res_v[:, pl.ds(pl.multiple_of(256 * a + 128 * h, 128), 128)] = value

    over(16, residual_step)
    res_copies = shrink(1, lambda a: res_v[:, 256 * a : 256 * a + 256])
    res_out = pltpu.make_async_copy(res_v, res_h, lsem.at[8])
    res_out.start()

    block, half_a = sub // 2, sub % 2
    side_c = (lane // 8) % 2
    codes = []
    for t in range(2):
        at = half_a * 4 + 2 * t + side_c
        code = jnp.where(block == 1, rows(ch_x, at), jnp.where(block == 2, rows(ch_y, at), rows(ch, at)))
        source = code // 8
        place = jnp.where(
            block == 1,
            jnp.where(source == 0, 1, jnp.where(source == 1, 0, 3)),
            jnp.where(block == 2, jnp.where(source == 0, 2, jnp.where(source == 1, 3, 0)), source),
        )
        codes.append((place, code % 8))

    def unpack(dense, odd):
        if odd:
            return jnp.where(left_c, roll(dense, -8), dense)
        return jnp.where(left_c, dense, roll(dense, 8))

    def assemble(n, copies, store):
        for copy in copies:
            copy.wait_recv()
        for a in range(8):
            from_x = unpack(pxr[n, a // 2], a % 2)
            from_y = unpack(pyr[n, a // 2], a % 2)
            one = jnp.broadcast_to(pd_r[n, a // 2, 0:1, :], (8, 128))
            two = jnp.broadcast_to(pd_r[n, a // 2, 1:2, :], (8, 128))
            from_d = unpack(jnp.where(block == 1, two, one), a % 2)
            for t in range(2):
                place, row = codes[t]
                value = jnp.where(place == 0, rows(zz[n, a], row), from_d)
                value = jnp.where(place == 1, rows(from_x, row), value)
                value = jnp.where(place == 2, rows(from_y, row), value)
                store(a, t, value)

    def store_q(a, t, value):
        eq[a, :, 128 * t : 128 * t + 128] = 0.25 * value

    def store_0(a, t, value):
        cols = slice(128 * t, 128 * t + 128)
        e0[a, :, cols] = value
        ea[a + 1, :, cols] = value

    def store_f(a, t, value):
        cols = slice(128 * t, 128 * t + 128)
        ef[a, :, cols] = ef[a, :, cols] + value

    def close(e):
        for t in range(2):
            cols = slice(128 * t, 128 * t + 128)
            e[0, :, cols] = jnp.where(half_a == 1, rows(e[8, :, cols], sub - half_a + 1 - half_a), 0.0)
            e[9, :, cols] = jnp.where(half_a == 0, rows(e[1, :, cols], sub - half_a + 1 - half_a), 0.0)

    def no_ghosts(a):
        return zero, (zero, zero)

    assemble(2, perm_copies, store_q)
    assemble(0, sol_copies, store_0)
    close(ea)

    def force_step(a):
        for h, (x, flux, _) in enumerate(stencil(ea, a, *no_ghosts(a))):
            cols = slice(128 * h, 128 * h + 128)
            ef[a, :, cols] = REACTION * x + eq[a, :, cols] * flux

    over(8, force_step)
    assemble(1, res_copies, store_f)

    for n, (source, target) in enumerate(((ea, eb), (eb, ea)) * (COARSE // 2)):
        if n:
            close(source)
        jacobi(source, ef, eq, no_ghosts, into(target), 8)

    parent_row = (pa // 8) * 2 + (pa % 8) // 4
    low_ob, low_oc = (pa // 2) % 2 == 0, pa % 2 == 0
    for a in range(8):
        one = rows(ea[a + 1, :, 0:128] - e0[a, :, 0:128], parent_row)
        two = rows(ea[a + 1, :, 128:256] - e0[a, :, 128:256], parent_row)
        value = jnp.where(low_ob, one, two)
        cor[a] = jnp.where(low_oc, value, roll(value, -8))
    spread = exact_dot(jnp.concatenate([cor[a] for a in range(8)], 0), upsample_m[...])
    for a in range(16):
        part = spread[8 * (a // 2) : 8 * (a // 2) + 8]
        va[a + 1] = vb[a + 1] + part

    copies2 = send_faces(2, va)
    take_faces(2, va, (va, vb), copies2)

    def into_result(a, h, value):
        sol_v[:, pl.ds(pl.multiple_of(256 * a + 128 * h, 128), 128)] = value

    jacobi(va, fr, qr, fine_ghosts, into(vb), 16)
    jacobi(vb, fr, qr, fine_ghosts, into(va), 16)
    jacobi(va, fr, qr, fine_ghosts, into_result, 16)
    sol_out = pltpu.make_async_copy(sol_v, sol_h, lsem.at[9])
    sol_out.start()

    for copy in (
        x_copies + msgs + [y_first, y_second] + copies0 + perm_copies + copies1 + sol_copies + res_copies + copies2
    ):
        copy.wait_send()
    res_out.wait()
    sol_out.wait()


def body(*args):
    count = 30
    vmem = lambda *shape: pltpu.VMEM(shape, F32)
    any_space = pl.BlockSpec(memory_space=pl.ANY)
    shape = jax.ShapeDtypeStruct((8, 4096), F32)
    return pl.pallas_call(
        kernel,
        out_shape=(shape, shape),
        in_specs=[any_space] * 8,
        out_specs=(any_space, any_space),
        scratch_shapes=[
            vmem(3, 8, 4096), vmem(3, 8, 4096),
            pltpu.SMEM((8,), I32), pltpu.SMEM((8,), I32), pltpu.SMEM((8,), I32), pltpu.SMEM((8,), I32),
            pltpu.VMEM((8, 6), I32), vmem(16, 128), vmem(4, 16, 128),
            vmem(32, 2, 128), vmem(32, 2, 128), vmem(32, 4, 128), vmem(32, 4, 128),
            vmem(18, 8, 256), vmem(18, 8, 256), vmem(16, 8, 256), vmem(16, 8, 256),
            vmem(16, 8, 128), vmem(16, 8, 256), vmem(16, 8, 128), vmem(16, 8, 256),
            vmem(3, 4, 8, 256), vmem(3, 4, 8, 256),
            vmem(3, 4, 8, 128), vmem(3, 4, 8, 128), vmem(3, 4, 8, 128),
            vmem(3, 4, 2, 128), vmem(3, 4, 2, 128),
            vmem(10, 8, 256), vmem(10, 8, 256), vmem(8, 8, 256), vmem(8, 8, 256), vmem(8, 8, 256),
            vmem(8, 8, 128), vmem(3, 8, 8, 128),
            pltpu.VMEM((256, 128), BF16), pltpu.VMEM((128, 256), BF16),
            vmem(8, 4096), vmem(8, 4096),
            pltpu.SemaphoreType.DMA((10,)), pltpu.SemaphoreType.DMA((count,)), pltpu.SemaphoreType.DMA((count,)),
        ],
        compiler_params=pltpu.CompilerParams(
            collective_id=0, has_side_effects=True, vmem_limit_bytes=32 * 1024 * 1024
        ),
    )(*args)


def solution(mesh):
    whole, flat = P(("gx", "gy"), None), P(("gx", "gy"))
    return jax.shard_map(
        body,
        mesh=mesh,
        in_specs=(whole, whole, whole, flat, flat, whole, flat, flat),
        out_specs=(whole, whole),
        check_vma=False,
    )
```

profile of v0, /device:TPU:1, one launch (start us, length us, event | category | flops | bytes accessed | tf_op | source)
XLA Modules:
  0.0 42.2 jit_solution(1555994435728074560)
XLA Ops:
  0.6 0.0 copy-start
  0.6 0.9 %copy-done = f32[8,4096]{1,0:T(8,128)S(1)} copy-done((f32[8,4096]{1,0:T(8,128)S(1)}, f32[8,4096]{1,0:T(8,128)}, u32[]{:S(2)}) %copy-start) | copy-done | bytes 131096
  1.5 0.0 copy-start.1
  1.5 0.9 %copy-done.1 = f32[8,4096]{1,0:T(8,128)S(1)} copy-done((f32[8,4096]{1,0:T(8,128)S(1)}, f32[8,4096]{1,0:T(8,128)}, u32[]{:S(2)}) %copy-start.1) | copy-done | bytes 131096
  2.4 0.0 copy-start.2
  2.4 0.9 %copy-done.2 = f32[8,4096]{1,0:T(8,128)S(1)} copy-done((f32[8,4096]{1,0:T(8,128)S(1)}, f32[8,4096]{1,0:T(8,128)}, u32[]{:S(2)}) %copy-start.2) | copy-done | bytes 131096
  3.3 0.0 copy-start.3
  3.3 0.7 %copy-done.3 = s32[8,6]{1,0:T(8,128)S(1)} copy-done((s32[8,6]{1,0:T(8,128)S(1)}, s32[8,6]{1,0:T(8,128)}, u32[]{:S(2)}) %copy-start.3) | copy-done | bytes 216
  4.0 0.0 copy-start.4
  4.0 0.7 %copy-done.4 = s32[8]{0:T(128)S(1)} copy-done((s32[8]{0:T(128)S(1)}, s32[8]{0:T(128)}, u32[]{:S(2)}) %copy-start.4) | copy-done | bytes 56
  4.7 0.0 copy-start.5
  4.7 0.7 %copy-done.5 = s32[8]{0:T(128)S(1)} copy-done((s32[8]{0:T(128)S(1)}, s32[8]{0:T(128)}, u32[]{:S(2)}) %copy-start.5) | copy-done | bytes 56
  5.3 0.0 copy-start.6
  5.3 0.7 %copy-done.6 = s32[8]{0:T(128)S(1)} copy-done((s32[8]{0:T(128)S(1)}, s32[8]{0:T(128)}, u32[]{:S(2)}) %copy-start.6) | copy-done | bytes 56
  6.0 0.0 copy-start.7
  6.0 0.7 %copy-done.7 = s32[8]{0:T(128)S(1)} copy-done((s32[8]{0:T(128)S(1)}, s32[8]{0:T(128)}, u32[]{:S(2)}) %copy-start.7) | copy-done | bytes 56
  6.7 34.2 %shard_map.95 = (f32[8,4096]{1,0:T(8,128)S(1)}, f32[8,4096]{1,0:T(8,128)S(1)}) custom-call(f32[8,4096]{1,0:T(8,128)S(1)} %copy-done, f32[8,4096]{1,0:T(8,128)S(1)} %copy-done.1, f32[8,4096]{1,0:T(8,128)S(1)} %copy-done.2, s32[8]{0:T(128)S(1)} %copy-done.4, s32[8]{0:T(128)S(1)} %copy-done.5, s32[8,6]{1,0:T(8,128)S(1)} %copy-done.3, s32[8]{0:T(128)S(1)} %copy-done.6, ...), custom_call_target="tpu_custom_call" | custom-call | tf_op jit(solution)/shard_map/pallas_call | solution.py:501
  40.9 0.7 %copy.12 = f32[8,4096]{1,0:T(8,128)} copy(f32[8,4096]{1,0:T(8,128)S(1)} %get-tuple-element.4) | data formatting | bytes 262144
  41.6 0.7 %copy.13 = f32[8,4096]{1,0:T(8,128)} copy(f32[8,4096]{1,0:T(8,128)S(1)} %get-tuple-element.5) | data formatting | bytes 262144
Async XLA Ops:
  0.6 0.9 %copy-start = (f32[8,4096]{1,0:T(8,128)S(1)}, f32[8,4096]{1,0:T(8,128)}, u32[]{:S(2)}) copy-start(f32[8,4096]{1,0:T(8,128)} %init_h.1) | copy-start | bytes 393220
  1.5 0.9 %copy-start.1 = (f32[8,4096]{1,0:T(8,128)S(1)}, f32[8,4096]{1,0:T(8,128)}, u32[]{:S(2)}) copy-start(f32[8,4096]{1,0:T(8,128)} %src_h.1) | copy-start | bytes 393220
  2.4 0.9 %copy-start.2 = (f32[8,4096]{1,0:T(8,128)S(1)}, f32[8,4096]{1,0:T(8,128)}, u32[]{:S(2)}) copy-start(f32[8,4096]{1,0:T(8,128)} %perm_h.1) | copy-start | bytes 393220
  3.3 0.7 %copy-start.3 = (s32[8,6]{1,0:T(8,128)S(1)}, s32[8,6]{1,0:T(8,128)}, u32[]{:S(2)}) copy-start(s32[8,6]{1,0:T(8,128)} %nb_h.1) | copy-start | bytes 580
  4.0 0.7 %copy-start.4 = (s32[8]{0:T(128)S(1)}, s32[8]{0:T(128)}, u32[]{:S(2)}) copy-start(s32[8]{0:T(128)} %mx_h.1) | copy-start | bytes 100
  4.7 0.7 %copy-start.5 = (s32[8]{0:T(128)S(1)}, s32[8]{0:T(128)}, u32[]{:S(2)}) copy-start(s32[8]{0:T(128)} %my_h.1) | copy-start | bytes 100
  5.3 0.7 %copy-start.6 = (s32[8]{0:T(128)S(1)}, s32[8]{0:T(128)}, u32[]{:S(2)}) copy-start(s32[8]{0:T(128)} %ch_h.1) | copy-start | bytes 100
  6.0 0.7 %copy-start.7 = (s32[8]{0:T(128)S(1)}, s32[8]{0:T(128)}, u32[]{:S(2)}) copy-start(s32[8]{0:T(128)} %pa_h.1) | copy-start | bytes 100
where the time goes:
time: 42.4 us; the launch traced here: 42.2 us
  Pallas kernels  34.2 us (81%)
  local copies, waits for them, and re-layouts  7.32 us (17%)
  between operations  0.66 us (2%)
    pallas_call x1, Pallas kernels, body(): pl.pallas_call(kernel, out_shape=(shape, shape), in_specs=[any_space] * 8...  34.2 us
    unnamed x18, local copies, waits for them, and re-layouts  7.32 us

commit v1 on v0

--- a/solution.py
+++ b/solution.py
@@ -50,13 +50,19 @@
     return out[:count] + (out[count : 2 * count] + out[2 * count :])
 
 
+def pairwise(x):
+    return ((x[0] + x[1]) + (x[2] + x[3])) + (x[4] + x[5])
+
+
 def kernel(
-    init_h, src_h, perm_h, mx_h, my_h, nb_h, ch_h, pa_h, sol_h, res_h,
+    init_h, src_h, perm_h, mx_h, my_h, nb_h, ch_h, pa_h, sol_v, res_v,
     own, px, t_mx, t_my, t_ch, t_pa, nbv, msg_s, msg_r, yi_s, yi_r, yf_s, yf_r,
-    va, vb, fr, qr, sb, sc, gb, gc, gs, gr, ps, pxr, pyr, pd_s, pd_r,
-    ea, eb, e0, ef, eq, cor, zz, restrict_m, upsample_m, sol_v, res_v,
+    vv, fr, qr, sb, sc, gb, gc, gs, gr, ps, pxr, pyr, pd_s, pd_r,
+    ee, e0, ef, eq, cor, zz, restrict_m, upsample_m,
     lsem, ssem, rsem,
 ):
+    va, vb = vv.at[0], vv.at[1]
+    ea, eb = ee.at[0], ee.at[1]
     i, j = lax.axis_index("gx"), lax.axis_index("gy")
     nx, ny = lax.axis_size("gx"), lax.axis_size("gy")
     xp = (i + 1 - 2 * (i % 2), j)
@@ -85,16 +91,14 @@
 
     used = [0]
 
-    def push(source, target, peer, there=None):
+    def push(source, target, peer):
         n = used[0]
-        if there is None:
-            there = n
-            used[0] += 1
+        used[0] += 1
         return pltpu.make_async_remote_copy(
             src_ref=source,
             dst_ref=target,
-            send_sem=ssem.at[n if there == n else n],
-            recv_sem=rsem.at[there],
+            send_sem=ssem.at[n],
+            recv_sem=rsem.at[n],
             device_id=peer,
             device_id_type=pl.DeviceIdType.MESH,
         )
@@ -113,11 +117,6 @@
             )
             for d in range(4)
         ]
-
-    pl.semaphore_wait(barrier, 5)
-    x_copies = [push(a, px.at[n], xp) for n, a in enumerate((init_h, src_h, perm_h))]
-    for copy in x_copies:
-        copy.start()
 
     lane = lax.broadcasted_iota(I32, (8, 128), 1)
     sub = lax.broadcasted_iota(I32, (8, 128), 0)
@@ -154,9 +153,6 @@
         wanted = wanted + jnp.where(hit, ((f ^ 1) * 8 + slot[f]).astype(F32), 0.0)
     msg_s[0:8, :] = jnp.broadcast_to(jnp.sum(wanted, axis=0, keepdims=True), (8, 128))
     msg_s[8:16, :] = ch.astype(F32)
-    msgs = push_around(lambda d: msg_s, lambda d: msg_r.at[d])
-    for copy in msgs:
-        copy.start()
 
     named = sub == t_my[0]
     for k in range(1, 8):
@@ -186,18 +182,27 @@
     same = (fine // 32 == small // 16) & ((fine % 16) // 2 == small % 16)
     upsample_m[...] = jnp.where(same, 1.0, 0.0).astype(BF16)
 
+    for copy in fields:
+        copy.wait()
+    pl.semaphore_wait(barrier, 5)
+    x_copies = [push(own.at[n], px.at[n], xp) for n in range(3)]
+    x_copies[0].start()
+    msgs = push_around(lambda d: msg_s, lambda d: msg_r.at[d])
+    for copy in msgs:
+        copy.start()
+    for copy in x_copies[1:]:
+        copy.start()
+
     def leaving(n, c):
         cols = pl.ds(128 * c, 128)
         return jnp.where(leave_own, rows(own[n, :, cols], leave_row), rows(px[n, :, cols], leave_row))
 
-    fields[0].wait()
     x_copies[0].wait_recv()
     for c in range(32):
         yi_s[c] = leaving(0, c)[0:2]
     y_first = push(yi_s, yi_r, yp)
     y_first.start()
     for n in (1, 2):
-        fields[n].wait()
         x_copies[n].wait_recv()
     for c in range(32):
         yf_s[c] = jnp.where(sub < 2, leaving(1, c), leaving(2, c))[0:4]
@@ -260,7 +265,21 @@
             copy.start()
         return copies
 
-    def take_faces(g, v, ends, copies):
+    def own_faces(v, ends):
+        for k in range(2):
+            cols = slice(128 * k, 128 * k + 128)
+            low = jnp.where(away[0] == 0, rows(v[16, :, cols], slot[0]), 0.0)
+            high = jnp.where(away[1] == 0, rows(v[1, :, cols], slot[1]), 0.0)
+            for end in ends:
+                end[0, :, cols] = low
+                end[17, :, cols] = high
+        for a in range(16):
+            gb[a] = rows(sb[a], row_b)
+            for h in range(2):
+                cols = slice(128 * h, 128 * h + 128)
+                gc[a, :, cols] = rows(sc[a, :, cols], row_c)
+
+    def take_faces(g, ends, copies):
         for copy in copies:
             copy.wait_recv()
         came = [[zero, zero] for _ in range(6)]
@@ -271,19 +290,19 @@
                     came[f][k] = jnp.where(away[f] == d + 1, got, came[f][k])
         for k in range(2):
             cols = slice(128 * k, 128 * k + 128)
-            low = jnp.where(away[0] == 0, rows(v[16, :, cols], slot[0]), came[0][k])
-            high = jnp.where(away[1] == 0, rows(v[1, :, cols], slot[1]), came[1][k])
+            low = jnp.where(away[0] == 0, ends[0][0, :, cols], came[0][k])
+            high = jnp.where(away[1] == 0, ends[0][17, :, cols], came[1][k])
             for end in ends:
                 end[0, :, cols] = low
                 end[17, :, cols] = high
         for a in range(16):
             both = jnp.where(group == a % 8, came[2][a // 8], came[3][a // 8])
-            gb[a] = jnp.where(here_b, rows(sb[a], row_b), roll(both, -16 * (a % 8)))
+            gb[a] = jnp.where(here_b, gb[a], roll(both, -16 * (a % 8)))
             for h in range(2):
                 cols = slice(128 * h, 128 * h + 128)
                 m, k = (2 * a + h) % 16, (2 * a + h) // 16
                 both = jnp.where(inside == m, came[4][k], came[5][k])
-                gc[a, :, cols] = jnp.where(here_c, rows(sc[a, :, cols], row_c), roll(both, -m))
+                gc[a, :, cols] = jnp.where(here_c, gc[a, :, cols], roll(both, -m))
 
     def stencil(v, a, ghost_b, ghost_c):
         x = [v[a + 1, :, 0:128], v[a + 1, :, 128:256]]
@@ -302,37 +321,37 @@
                 v[a + 2, :, cols],
             )
             mobility = 1.0 + x[h] * x[h]
-            squares, flux = 6.0 * mobility, None
-            for w in beside:
-                square = w * w
-                squares = squares + square
-                term = (mobility + square) * (x[h] - w)
-                flux = term if flux is None else flux + term
+            square = [w * w for w in beside]
+            term = [(mobility + y) * (x[h] - w) for y, w in zip(square, beside)]
+            squares = 6.0 * mobility + pairwise(square)
+            flux = pairwise(term)
             out.append((x[h], flux, squares))
         return out
 
     def fine_ghosts(a):
         return gb[a], (gc[a, :, 0:128], gc[a, :, 128:256])
 
-    def over(count, step):
-        lax.fori_loop(0, count, lambda a, carry: (step(a), carry)[1], 0, unroll=4)
-
     def jacobi(v, force, coefficient, ghosts, store, count):
-        def step(a):
+        for a in range(count):
             parts = stencil(v, a, *ghosts(a))
             for h, (x, flux, conduct) in enumerate(parts):
                 cols = slice(128 * h, 128 * h + 128)
                 q = coefficient[a, :, cols]
                 defect = force[a, :, cols] - (REACTION * x + q * flux)
-                store(a, h, x + DAMPING * defect / (REACTION + q * conduct))
-
-        over(count, step)
+                store(a, h, x + defect * (DAMPING / (REACTION + q * conduct)))
 
     def into(ref):
         def store(a, h, value):
             ref[a + 1, :, 128 * h : 128 * h + 128] = value
 
         return store
+
+    def smooth(sweeps):
+        def sweep(n, carry):
+            jacobi(vv.at[n % 2], fr, qr, fine_ghosts, into(vv.at[(n + 1) % 2]), 16)
+            return carry
+
+        lax.fori_loop(0, sweeps, sweep, 0)
 
     def shrink(n, layer):
         fold = jnp.concatenate([layer(2 * a) + layer(2 * a + 1) for a in range(8)], 0)
@@ -362,31 +381,30 @@
     for c in range(32):
         va[1 + c // 2, :, 128 * (c % 2) : 128 * (c % 2) + 128] = arrived(0, yi_r, 0, c)
     copies0 = send_faces(0, va)
+    own_faces(va, (va, vb))
     y_second.wait_recv()
     for c in range(32):
         cols = slice(128 * (c % 2), 128 * (c % 2) + 128)
         fr[c // 2, :, cols] = arrived(1, yf_r, 0, c)
         qr[c // 2, :, cols] = 0.5 * arrived(2, yf_r, 2, c)
     perm_copies = shrink(2, lambda a: qr[a])
-    take_faces(0, va, (va, vb), copies0)
-
-    for source, target in ((va, vb), (vb, va), (va, vb)):
-        jacobi(source, fr, qr, fine_ghosts, into(target), 16)
+    take_faces(0, (va, vb), copies0)
+    smooth(INNER)
 
     copies1 = send_faces(1, vb)
+    own_faces(vb, (vb,))
     sol_copies = shrink(0, lambda a: vb[a + 1])
-    take_faces(1, vb, (vb,), copies1)
-
-    def residual_step(a):
+    take_faces(1, (vb,), copies1)
+
+    layers = []
+    for a in range(16):
+        layers.append([])
         for h, (x, flux, _) in enumerate(stencil(vb, a, *fine_ghosts(a))):
             cols = slice(128 * h, 128 * h + 128)
             value = fr[a, :, cols] - (REACTION * x + qr[a, :, cols] * flux)
-            res_v[:, pl.ds(pl.multiple_of(256 * a + 128 * h, 128), 128)] = value
-
-    over(16, residual_step)
-    res_copies = shrink(1, lambda a: res_v[:, 256 * a : 256 * a + 256])
-    res_out = pltpu.make_async_copy(res_v, res_h, lsem.at[8])
-    res_out.start()
+            res_v[:, 256 * a + 128 * h : 256 * a + 128 * h + 128] = value
+            layers[a].append(value)
+    res_copies = shrink(1, lambda a: jnp.concatenate(layers[a], 1))
 
     block, half_a = sub // 2, sub % 2
     side_c = (lane // 8) % 2
@@ -448,18 +466,19 @@
     assemble(0, sol_copies, store_0)
     close(ea)
 
-    def force_step(a):
+    for a in range(8):
         for h, (x, flux, _) in enumerate(stencil(ea, a, *no_ghosts(a))):
             cols = slice(128 * h, 128 * h + 128)
             ef[a, :, cols] = REACTION * x + eq[a, :, cols] * flux
-
-    over(8, force_step)
     assemble(1, res_copies, store_f)
 
-    for n, (source, target) in enumerate(((ea, eb), (eb, ea)) * (COARSE // 2)):
-        if n:
-            close(source)
+    def coarse_sweep(n, carry):
+        source, target = ee.at[n % 2], ee.at[(n + 1) % 2]
         jacobi(source, ef, eq, no_ghosts, into(target), 8)
+        close(target)
+        return carry
+
+    lax.fori_loop(0, COARSE, coarse_sweep, 0)
 
     parent_row = (pa // 8) * 2 + (pa % 8) // 4
     low_ob, low_oc = (pa // 2) % 2 == 0, pa % 2 == 0
@@ -474,55 +493,49 @@
         va[a + 1] = vb[a + 1] + part
 
     copies2 = send_faces(2, va)
-    take_faces(2, va, (va, vb), copies2)
+    own_faces(va, (va, vb))
+    take_faces(2, (va, vb), copies2)
 
     def into_result(a, h, value):
-        sol_v[:, pl.ds(pl.multiple_of(256 * a + 128 * h, 128), 128)] = value
-
-    jacobi(va, fr, qr, fine_ghosts, into(vb), 16)
-    jacobi(vb, fr, qr, fine_ghosts, into(va), 16)
+        sol_v[:, 256 * a + 128 * h : 256 * a + 128 * h + 128] = value
+
+    smooth(INNER - 1)
     jacobi(va, fr, qr, fine_ghosts, into_result, 16)
-    sol_out = pltpu.make_async_copy(sol_v, sol_h, lsem.at[9])
-    sol_out.start()
 
     for copy in (
         x_copies + msgs + [y_first, y_second] + copies0 + perm_copies + copies1 + sol_copies + res_copies + copies2
     ):
         copy.wait_send()
-    res_out.wait()
-    sol_out.wait()
 
 
 def body(*args):
     count = 30
     vmem = lambda *shape: pltpu.VMEM(shape, F32)
     any_space = pl.BlockSpec(memory_space=pl.ANY)
-    shape = jax.ShapeDtypeStruct((8, 4096), F32)
     return pl.pallas_call(
         kernel,
-        out_shape=(shape, shape),
+        out_shape=(pltpu.VMEM((8, 4096), F32), pltpu.VMEM((8, 4096), F32)),
         in_specs=[any_space] * 8,
-        out_specs=(any_space, any_space),
+        out_specs=(pl.BlockSpec(memory_space=pltpu.VMEM),) * 2,
         scratch_shapes=[
             vmem(3, 8, 4096), vmem(3, 8, 4096),
             pltpu.SMEM((8,), I32), pltpu.SMEM((8,), I32), pltpu.SMEM((8,), I32), pltpu.SMEM((8,), I32),
             pltpu.VMEM((8, 6), I32), vmem(16, 128), vmem(4, 16, 128),
             vmem(32, 2, 128), vmem(32, 2, 128), vmem(32, 4, 128), vmem(32, 4, 128),
-            vmem(18, 8, 256), vmem(18, 8, 256), vmem(16, 8, 256), vmem(16, 8, 256),
+            vmem(2, 18, 8, 256), vmem(16, 8, 256), vmem(16, 8, 256),
             vmem(16, 8, 128), vmem(16, 8, 256), vmem(16, 8, 128), vmem(16, 8, 256),
             vmem(3, 4, 8, 256), vmem(3, 4, 8, 256),
             vmem(3, 4, 8, 128), vmem(3, 4, 8, 128), vmem(3, 4, 8, 128),
             vmem(3, 4, 2, 128), vmem(3, 4, 2, 128),
-            vmem(10, 8, 256), vmem(10, 8, 256), vmem(8, 8, 256), vmem(8, 8, 256), vmem(8, 8, 256),
+            vmem(2, 10, 8, 256), vmem(8, 8, 256), vmem(8, 8, 256), vmem(8, 8, 256),
             vmem(8, 8, 128), vmem(3, 8, 8, 128),
             pltpu.VMEM((256, 128), BF16), pltpu.VMEM((128, 256), BF16),
-            vmem(8, 4096), vmem(8, 4096),
             pltpu.SemaphoreType.DMA((10,)), pltpu.SemaphoreType.DMA((count,)), pltpu.SemaphoreType.DMA((count,)),
         ],
         compiler_params=pltpu.CompilerParams(
             collective_id=0, has_side_effects=True, vmem_limit_bytes=32 * 1024 * 1024
         ),
-    )(*args)
+    )(*[pltpu.with_memory_space_constraint(a, pltpu.HBM) for a in args])
 
 
 def solution(mesh):

time: 42.4 us -> 34.8 us (0.82)
  local copies, waits for them, and re-layouts: 7.32 us -> 1.31 us
  Pallas kernels: 34.2 us -> 32.8 us
    unnamed x18 -> x2, local copies, waits for them, and re-layouts: 7.32 us -> 1.31 us
    pallas_call x1, Pallas kernels: 34.2 us -> 32.8 us  [body(): pl.pallas_call(kernel, out_shape=(pltpu.VMEM((8, 4096), F32), pltpu.VMEM(...]
where the time goes in v1:
time: 34.8 us; the launch traced here: 34.7 us
  Pallas kernels  32.8 us (94%)
  local copies, waits for them, and re-layouts  1.31 us (4%)
  between operations  0.64 us (2%)
    pallas_call x1, Pallas kernels, body(): pl.pallas_call(kernel, out_shape=(pltpu.VMEM((8, 4096), F32), pltpu.VMEM(...  32.8 us
    unnamed x2, local copies, waits for them, and re-layouts  1.31 us

profile of v1, /device:TPU:1, one launch (start us, length us, event | category | flops | bytes accessed | tf_op | source)
XLA Modules:
  0.0 34.7 jit_solution(13052478837750509079)
XLA Ops:
  0.6 32.8 %shard_map.95 = (f32[8,4096]{1,0:T(8,128)S(1)}, f32[8,4096]{1,0:T(8,128)S(1)}) custom-call(f32[8,4096]{1,0:T(8,128)} %init_h.1, f32[8,4096]{1,0:T(8,128)} %src_h.1, f32[8,4096]{1,0:T(8,128)} %perm_h.1, s32[8]{0:T(128)} %mx_h.1, s32[8]{0:T(128)} %my_h.1, s32[8,6]{1,0:T(8,128)} %nb_h.1, s32[8]{0:T(128)} %ch_h.1, s32[8]{0:T(128)} %pa_h.1), custom_call_target="tpu_custom_call" | custom-call | tf_op jit(solution)/shard_map/pallas_call | solution.py:515
  33.4 0.7 %copy.12 = f32[8,4096]{1,0:T(8,128)} copy(f32[8,4096]{1,0:T(8,128)S(1)} %get-tuple-element.2) | data formatting | bytes 262144
  34.1 0.7 %copy.13 = f32[8,4096]{1,0:T(8,128)} copy(f32[8,4096]{1,0:T(8,128)S(1)} %get-tuple-element.3) | data formatting | bytes 262144

commit v2 on v1

--- a/solution.py
+++ b/solution.py
@@ -55,24 +55,21 @@
 
 
 def kernel(
-    init_h, src_h, perm_h, mx_h, my_h, nb_h, ch_h, pa_h, sol_v, res_v,
+    init_h, src_h, perm_h, mx_h, my_h, nb_h, ch_h, pa_h, both_v,
     own, px, t_mx, t_my, t_ch, t_pa, nbv, msg_s, msg_r, yi_s, yi_r, yf_s, yf_r,
-    vv, fr, qr, sb, sc, gb, gc, gs, gr, ps, pxr, pyr, pd_s, pd_r,
-    ee, e0, ef, eq, cor, zz, restrict_m, upsample_m,
-    lsem, ssem, rsem,
+    vv, fr, qr, sb, sc, gb, gc, every_s, every_r, gs, gr, ps, pxr, pyr, pd_s, pd_r,
+    e0, ef, eq, cor, zz, restrict_m, upsample_m,
+    ready, lsem, ssem, rsem,
 ):
     va, vb = vv.at[0], vv.at[1]
-    ea, eb = ee.at[0], ee.at[1]
     i, j = lax.axis_index("gx"), lax.axis_index("gy")
     nx, ny = lax.axis_size("gx"), lax.axis_size("gy")
     xp = (i + 1 - 2 * (i % 2), j)
     yp = (i, j + 1 - 2 * (j % 2))
     diag = (xp[0], yp[1])
+    beyond_x = ((i + nx - 1 + 2 * (i % 2)) % nx, j)
+    beyond_y = (i, (j + ny - 1 + 2 * (j % 2)) % ny)
     around = (((i + nx - 1) % nx, j), ((i + 1) % nx, j), (i, (j + ny - 1) % ny), (i, (j + 1) % ny))
-
-    barrier = pltpu.get_barrier_semaphore()
-    for peer in around + (diag,):
-        pl.semaphore_signal(barrier, inc=1, device_id=peer, device_id_type=pl.DeviceIdType.MESH)
 
     tables = [
         pltpu.make_async_copy(a, b, lsem.at[n])
@@ -89,6 +86,27 @@
     for copy in fields:
         copy.start()
 
+    even = (i + j) % 2 == 0
+    odd = (i + j) % 2 == 1
+    barrier = pltpu.get_barrier_semaphore()
+
+    def signal(semaphore, peer):
+        pl.semaphore_signal(semaphore, inc=1, device_id=peer, device_id_type=pl.DeviceIdType.MESH)
+
+    @pl.when(even)
+    def _():
+        signal(barrier, beyond_x)
+        signal(barrier, beyond_y)
+        pl.semaphore_wait(barrier, 2)
+        signal(ready.at[0], xp)
+        signal(ready.at[1], yp)
+
+    @pl.when(odd)
+    def _():
+        signal(barrier, xp)
+        signal(barrier, yp)
+        pl.semaphore_wait(ready.at[0], 1)
+
     used = [0]
 
     def push(source, target, peer):
@@ -118,6 +136,10 @@
             for d in range(4)
         ]
 
+    x_copies = [push(a, px.at[n], xp) for n, a in enumerate((init_h, src_h, perm_h))]
+    for copy in x_copies:
+        copy.start()
+
     lane = lax.broadcasted_iota(I32, (8, 128), 1)
     sub = lax.broadcasted_iota(I32, (8, 128), 0)
     zero = jnp.zeros((8, 128), F32)
@@ -136,24 +158,6 @@
     links = [jnp.broadcast_to(nbv[:, f : f + 1], (8, 128)) for f in range(6)]
     away = [jnp.where(c >= 0, c // 8, 7) for c in links]
     slot = [jnp.where(c >= 0, c % 8, 0) for c in links]
-    marks = jnp.concatenate([(lane == d).astype(F32) for d in away], 0)
-    before = (
-        lax.broadcasted_iota(I32, (48, 48), 1) < lax.broadcasted_iota(I32, (48, 48), 0)
-    ).astype(F32)
-    counts = jnp.dot(before, marks, preferred_element_type=F32)
-    rank = []
-    wanted = zero
-    for f in range(6):
-        mine = jnp.where(lane == away[f], counts[8 * f : 8 * f + 8], 0.0)
-        place = jnp.broadcast_to(jnp.sum(mine, axis=1, keepdims=True), (8, 128)).astype(I32)
-        place = jnp.minimum(place, 7)
-        rank.append(place)
-        remote = (away[f] >= 1) & (away[f] <= 4)
-        hit = (lane == away[f] * 8 + place) & remote
-        wanted = wanted + jnp.where(hit, ((f ^ 1) * 8 + slot[f]).astype(F32), 0.0)
-    msg_s[0:8, :] = jnp.broadcast_to(jnp.sum(wanted, axis=0, keepdims=True), (8, 128))
-    msg_s[8:16, :] = ch.astype(F32)
-
     named = sub == t_my[0]
     for k in range(1, 8):
         named = named | (sub == t_my[k])
@@ -173,51 +177,35 @@
         order = order + jnp.where((entry >= 8) & (my > entry), 1, 0)
     final_first = order == 0
 
-    fine = lax.broadcasted_iota(I32, (256, 128), 0)
-    small = lax.broadcasted_iota(I32, (256, 128), 1)
-    same = (fine // 32 == small // 16) & ((fine % 16) // 2 == small % 8)
-    restrict_m[...] = jnp.where(same, 0.125, 0.0).astype(BF16)
-    fine = lax.broadcasted_iota(I32, (128, 256), 1)
-    small = lax.broadcasted_iota(I32, (128, 256), 0)
-    same = (fine // 32 == small // 16) & ((fine % 16) // 2 == small % 16)
-    upsample_m[...] = jnp.where(same, 1.0, 0.0).astype(BF16)
-
-    for copy in fields:
-        copy.wait()
-    pl.semaphore_wait(barrier, 5)
-    x_copies = [push(own.at[n], px.at[n], xp) for n in range(3)]
-    x_copies[0].start()
-    msgs = push_around(lambda d: msg_s, lambda d: msg_r.at[d])
-    for copy in msgs:
-        copy.start()
-    for copy in x_copies[1:]:
-        copy.start()
-
     def leaving(n, c):
         cols = pl.ds(128 * c, 128)
         return jnp.where(leave_own, rows(own[n, :, cols], leave_row), rows(px[n, :, cols], leave_row))
 
+    fields[0].wait()
     x_copies[0].wait_recv()
     for c in range(32):
         yi_s[c] = leaving(0, c)[0:2]
     y_first = push(yi_s, yi_r, yp)
+
+    @pl.when(odd)
+    def _():
+        pl.semaphore_wait(ready.at[1], 1)
+
     y_first.start()
+
+    @pl.when(odd)
+    def _():
+        pl.semaphore_wait(barrier, 2)
+        signal(ready.at[2], beyond_x)
+        signal(ready.at[3], beyond_y)
+
     for n in (1, 2):
+        fields[n].wait()
         x_copies[n].wait_recv()
     for c in range(32):
         yf_s[c] = jnp.where(sub < 2, leaving(1, c), leaving(2, c))[0:4]
     y_second = push(yf_s, yf_r, yp)
     y_second.start()
-
-    for copy in msgs:
-        copy.wait_recv()
-    give = []
-    for d in range(4):
-        code = jnp.where(lane == (OPP[d] + 1) * 8 + sub, msg_r[d, 0:8, :], 0.0)
-        code = jnp.broadcast_to(jnp.sum(code, axis=1, keepdims=True), (8, 128)).astype(I32)
-        give.append((code // 8, code % 8))
-    ch_x = msg_r[1 - i % 2, 8:16, :].astype(I32)
-    ch_y = msg_r[3 - j % 2, 8:16, :].astype(I32)
 
     def arrived(n, ref, top, c):
         cols = pl.ds(128 * c, 128)
@@ -235,7 +223,7 @@
     row_c = jnp.where(left_c, slot[4], slot[5])
     here_c = jnp.where(left_c, away[4], away[5]) == 0
 
-    def send_faces(g, v):
+    def pack_faces(v):
         packed = [[v[1, :, 0:128], v[1, :, 128:256]], [v[16, :, 0:128], v[16, :, 128:256]]]
         for _ in range(4):
             packed.append([zero, zero])
@@ -253,14 +241,18 @@
                 moved = roll(both, m)
                 packed[5][k] = jnp.where(inside == m, moved, packed[5][k])
                 packed[4][k] = jnp.where(inside == (m + 15) % 16, moved, packed[4][k])
+        return packed
+
+    def send_faces(g, v):
+        packed = pack_faces(v)
         for d in range(4):
             face, row = give[d]
             for k in range(2):
                 out = rows(packed[0][k], row)
                 for f in range(1, 6):
                     out = jnp.where(face == f, rows(packed[f][k], row), out)
-                gs[g, d, :, 128 * k : 128 * k + 128] = out
-        copies = push_around(lambda d: gs.at[g, d], lambda d: gr.at[g, d])
+                gs[g - 1, d, :, 128 * k : 128 * k + 128] = out
+        copies = push_around(lambda d: gs.at[g - 1, d], lambda d: gr.at[g - 1, d])
         for copy in copies:
             copy.start()
         return copies
@@ -279,15 +271,14 @@
                 cols = slice(128 * h, 128 * h + 128)
                 gc[a, :, cols] = rows(sc[a, :, cols], row_c)
 
-    def take_faces(g, ends, copies):
+    def take_faces(got, ends, copies):
         for copy in copies:
             copy.wait_recv()
         came = [[zero, zero] for _ in range(6)]
         for f in range(6):
             for k in range(2):
                 for d in range(4):
-                    got = rows(gr[g, d, :, 128 * k : 128 * k + 128], rank[f])
-                    came[f][k] = jnp.where(away[f] == d + 1, got, came[f][k])
+                    came[f][k] = jnp.where(away[f] == d + 1, got(d, f, slice(128 * k, 128 * k + 128)), came[f][k])
         for k in range(2):
             cols = slice(128 * k, 128 * k + 128)
             low = jnp.where(away[0] == 0, ends[0][0, :, cols], came[0][k])
@@ -304,8 +295,10 @@
                 both = jnp.where(inside == m, came[4][k], came[5][k])
                 gc[a, :, cols] = jnp.where(here_c, gc[a, :, cols], roll(both, -m))
 
-    def stencil(v, a, ghost_b, ghost_c):
-        x = [v[a + 1, :, 0:128], v[a + 1, :, 128:256]]
+    def halves(v, a):
+        return [v[a, :, 0:128], v[a, :, 128:256]]
+
+    def parts(before, x, after, ghost_b, ghost_c):
         down, up = [roll(y, 16) for y in x], [roll(y, -16) for y in x]
         beside_b = (
             (jnp.where(low_b, ghost_b, down[0]), jnp.where(high_b, up[1], up[0])),
@@ -313,12 +306,11 @@
         )
         out = []
         for h in range(2):
-            cols = slice(128 * h, 128 * h + 128)
             beside = beside_b[h] + (
                 jnp.where(low_c, ghost_c[h], roll(x[h], 1)),
                 jnp.where(high_c, ghost_c[h], roll(x[h], -1)),
-                v[a, :, cols],
-                v[a + 2, :, cols],
+                before[h],
+                after[h],
             )
             mobility = 1.0 + x[h] * x[h]
             square = [w * w for w in beside]
@@ -328,13 +320,15 @@
             out.append((x[h], flux, squares))
         return out
 
+    def stencil(v, a, ghost_b, ghost_c):
+        return parts(halves(v, a), halves(v, a + 1), halves(v, a + 2), ghost_b, ghost_c)
+
     def fine_ghosts(a):
         return gb[a], (gc[a, :, 0:128], gc[a, :, 128:256])
 
     def jacobi(v, force, coefficient, ghosts, store, count):
         for a in range(count):
-            parts = stencil(v, a, *ghosts(a))
-            for h, (x, flux, conduct) in enumerate(parts):
+            for h, (x, flux, conduct) in enumerate(stencil(v, a, *ghosts(a))):
                 cols = slice(128 * h, 128 * h + 128)
                 q = coefficient[a, :, cols]
                 defect = force[a, :, cols] - (REACTION * x + q * flux)
@@ -347,11 +341,8 @@
         return store
 
     def smooth(sweeps):
-        def sweep(n, carry):
+        for n in range(sweeps):
             jacobi(vv.at[n % 2], fr, qr, fine_ghosts, into(vv.at[(n + 1) % 2]), 16)
-            return carry
-
-        lax.fori_loop(0, sweeps, sweep, 0)
 
     def shrink(n, layer):
         fold = jnp.concatenate([layer(2 * a) + layer(2 * a + 1) for a in range(8)], 0)
@@ -380,21 +371,78 @@
     y_first.wait_recv()
     for c in range(32):
         va[1 + c // 2, :, 128 * (c % 2) : 128 * (c % 2) + 128] = arrived(0, yi_r, 0, c)
-    copies0 = send_faces(0, va)
+    packed = pack_faces(va)
+    for f in range(6):
+        for k in range(2):
+            every_s[f, :, 128 * k : 128 * k + 128] = packed[f][k]
+
+    @pl.when(even)
+    def _():
+        pl.semaphore_wait(ready.at[2], 1)
+        pl.semaphore_wait(ready.at[3], 1)
+
+    copies0 = push_around(lambda d: every_s, lambda d: every_r.at[d])
+    for copy in copies0:
+        copy.start()
     own_faces(va, (va, vb))
+
+    marks = jnp.concatenate([(lane == d).astype(F32) for d in away], 0)
+    before = (
+        lax.broadcasted_iota(I32, (48, 48), 1) < lax.broadcasted_iota(I32, (48, 48), 0)
+    ).astype(F32)
+    counts = jnp.dot(before, marks, preferred_element_type=F32)
+    rank = []
+    wanted = zero
+    for f in range(6):
+        mine = jnp.where(lane == away[f], counts[8 * f : 8 * f + 8], 0.0)
+        place = jnp.broadcast_to(jnp.sum(mine, axis=1, keepdims=True), (8, 128)).astype(I32)
+        place = jnp.minimum(place, 7)
+        rank.append(place)
+        remote = (away[f] >= 1) & (away[f] <= 4)
+        hit = (lane == away[f] * 8 + place) & remote
+        wanted = wanted + jnp.where(hit, ((f ^ 1) * 8 + slot[f]).astype(F32), 0.0)
+    msg_s[0:8, :] = jnp.broadcast_to(jnp.sum(wanted, axis=0, keepdims=True), (8, 128))
+    msg_s[8:16, :] = ch.astype(F32)
+
+    msgs = push_around(lambda d: msg_s, lambda d: msg_r.at[d])
+    for copy in msgs:
+        copy.start()
+
+    fine = lax.broadcasted_iota(I32, (256, 128), 0)
+    small = lax.broadcasted_iota(I32, (256, 128), 1)
+    same = (fine // 32 == small // 16) & ((fine % 16) // 2 == small % 8)
+    restrict_m[...] = jnp.where(same, 0.125, 0.0).astype(BF16)
+    fine = lax.broadcasted_iota(I32, (128, 256), 1)
+    small = lax.broadcasted_iota(I32, (128, 256), 0)
+    same = (fine // 32 == small // 16) & ((fine % 16) // 2 == small % 16)
+    upsample_m[...] = jnp.where(same, 1.0, 0.0).astype(BF16)
+
     y_second.wait_recv()
     for c in range(32):
         cols = slice(128 * (c % 2), 128 * (c % 2) + 128)
         fr[c // 2, :, cols] = arrived(1, yf_r, 0, c)
         qr[c // 2, :, cols] = 0.5 * arrived(2, yf_r, 2, c)
     perm_copies = shrink(2, lambda a: qr[a])
-    take_faces(0, (va, vb), copies0)
+    take_faces(lambda d, f, cols: rows(every_r[d, f ^ 1, :, cols], slot[f]), (va, vb), copies0)
     smooth(INNER)
+
+    for copy in msgs:
+        copy.wait_recv()
+    give = []
+    for d in range(4):
+        code = jnp.where(lane == (OPP[d] + 1) * 8 + sub, msg_r[d, 0:8, :], 0.0)
+        code = jnp.broadcast_to(jnp.sum(code, axis=1, keepdims=True), (8, 128)).astype(I32)
+        give.append((code // 8, code % 8))
+    ch_x = msg_r[1 - i % 2, 8:16, :].astype(I32)
+    ch_y = msg_r[3 - j % 2, 8:16, :].astype(I32)
+
+    def asked(g):
+        return lambda d, f, cols: rows(gr[g - 1, d, :, cols], rank[f])
 
     copies1 = send_faces(1, vb)
     own_faces(vb, (vb,))
     sol_copies = shrink(0, lambda a: vb[a + 1])
-    take_faces(1, (vb,), copies1)
+    take_faces(asked(1), (vb,), copies1)
 
     layers = []
     for a in range(16):
@@ -402,7 +450,7 @@
         for h, (x, flux, _) in enumerate(stencil(vb, a, *fine_ghosts(a))):
             cols = slice(128 * h, 128 * h + 128)
             value = fr[a, :, cols] - (REACTION * x + qr[a, :, cols] * flux)
-            res_v[:, 256 * a + 128 * h : 256 * a + 128 * h + 128] = value
+            both_v[8:16, 256 * a + 128 * h : 256 * a + 128 * h + 128] = value
             layers[a].append(value)
     res_copies = shrink(1, lambda a: jnp.concatenate(layers[a], 1))
 
@@ -444,47 +492,48 @@
     def store_q(a, t, value):
         eq[a, :, 128 * t : 128 * t + 128] = 0.25 * value
 
+    coarse = [[None, None] for _ in range(8)]
+
     def store_0(a, t, value):
-        cols = slice(128 * t, 128 * t + 128)
-        e0[a, :, cols] = value
-        ea[a + 1, :, cols] = value
+        coarse[a][t] = value
 
     def store_f(a, t, value):
         cols = slice(128 * t, 128 * t + 128)
         ef[a, :, cols] = ef[a, :, cols] + value
 
-    def close(e):
-        for t in range(2):
-            cols = slice(128 * t, 128 * t + 128)
-            e[0, :, cols] = jnp.where(half_a == 1, rows(e[8, :, cols], sub - half_a + 1 - half_a), 0.0)
-            e[9, :, cols] = jnp.where(half_a == 0, rows(e[1, :, cols], sub - half_a + 1 - half_a), 0.0)
-
-    def no_ghosts(a):
-        return zero, (zero, zero)
+    def coarse_parts(e):
+        other = sub + 1 - 2 * half_a
+        below = [jnp.where(half_a == 1, rows(e[7][t], other), 0.0) for t in range(2)]
+        above = [jnp.where(half_a == 0, rows(e[0][t], other), 0.0) for t in range(2)]
+        layers = [below] + e + [above]
+        return [parts(*layers[a : a + 3], zero, (zero, zero)) for a in range(8)]
 
     assemble(2, perm_copies, store_q)
     assemble(0, sol_copies, store_0)
-    close(ea)
-
-    for a in range(8):
-        for h, (x, flux, _) in enumerate(stencil(ea, a, *no_ghosts(a))):
+    for a, part in enumerate(coarse_parts(coarse)):
+        for h, (x, flux, _) in enumerate(part):
             cols = slice(128 * h, 128 * h + 128)
+            e0[a, :, cols] = x
             ef[a, :, cols] = REACTION * x + eq[a, :, cols] * flux
     assemble(1, res_copies, store_f)
 
-    def coarse_sweep(n, carry):
-        source, target = ee.at[n % 2], ee.at[(n + 1) % 2]
-        jacobi(source, ef, eq, no_ghosts, into(target), 8)
-        close(target)
-        return carry
-
-    lax.fori_loop(0, COARSE, coarse_sweep, 0)
+    iterate = coarse
+    for repeat in range(COARSE):
+        after = []
+        for a, part in enumerate(coarse_parts(iterate)):
+            after.append([])
+            for h, (x, flux, conduct) in enumerate(part):
+                cols = slice(128 * h, 128 * h + 128)
+                q = eq[a, :, cols]
+                defect = ef[a, :, cols] - (REACTION * x + q * flux)
+                after[a].append(x + defect * (DAMPING / (REACTION + q * conduct)))
+        iterate = after
 
     parent_row = (pa // 8) * 2 + (pa % 8) // 4
     low_ob, low_oc = (pa // 2) % 2 == 0, pa % 2 == 0
     for a in range(8):
-        one = rows(ea[a + 1, :, 0:128] - e0[a, :, 0:128], parent_row)
-        two = rows(ea[a + 1, :, 128:256] - e0[a, :, 128:256], parent_row)
+        one = rows(iterate[a][0] - e0[a, :, 0:128], parent_row)
+        two = rows(iterate[a][1] - e0[a, :, 128:256], parent_row)
         value = jnp.where(low_ob, one, two)
         cor[a] = jnp.where(low_oc, value, roll(value, -8))
     spread = exact_dot(jnp.concatenate([cor[a] for a in range(8)], 0), upsample_m[...])
@@ -494,10 +543,10 @@
 
     copies2 = send_faces(2, va)
     own_faces(va, (va, vb))
-    take_faces(2, (va, vb), copies2)
+    take_faces(asked(2), (va, vb), copies2)
 
     def into_result(a, h, value):
-        sol_v[:, 256 * a + 128 * h : 256 * a + 128 * h + 128] = value
+        both_v[0:8, 256 * a + 128 * h : 256 * a + 128 * h + 128] = value
 
     smooth(INNER - 1)
     jacobi(va, fr, qr, fine_ghosts, into_result, 16)
@@ -512,11 +561,11 @@
     count = 30
     vmem = lambda *shape: pltpu.VMEM(shape, F32)
     any_space = pl.BlockSpec(memory_space=pl.ANY)
-    return pl.pallas_call(
+    both = pl.pallas_call(
         kernel,
-        out_shape=(pltpu.VMEM((8, 4096), F32), pltpu.VMEM((8, 4096), F32)),
+        out_shape=pltpu.VMEM((16, 4096), F32),
         in_specs=[any_space] * 8,
-        out_specs=(pl.BlockSpec(memory_space=pltpu.VMEM),) * 2,
+        out_specs=pl.BlockSpec(memory_space=pltpu.VMEM),
         scratch_shapes=[
             vmem(3, 8, 4096), vmem(3, 8, 4096),
             pltpu.SMEM((8,), I32), pltpu.SMEM((8,), I32), pltpu.SMEM((8,), I32), pltpu.SMEM((8,), I32),
@@ -524,18 +573,19 @@
             vmem(32, 2, 128), vmem(32, 2, 128), vmem(32, 4, 128), vmem(32, 4, 128),
             vmem(2, 18, 8, 256), vmem(16, 8, 256), vmem(16, 8, 256),
             vmem(16, 8, 128), vmem(16, 8, 256), vmem(16, 8, 128), vmem(16, 8, 256),
-            vmem(3, 4, 8, 256), vmem(3, 4, 8, 256),
+            vmem(6, 8, 256), vmem(4, 6, 8, 256), vmem(2, 4, 8, 256), vmem(2, 4, 8, 256),
             vmem(3, 4, 8, 128), vmem(3, 4, 8, 128), vmem(3, 4, 8, 128),
             vmem(3, 4, 2, 128), vmem(3, 4, 2, 128),
-            vmem(2, 10, 8, 256), vmem(8, 8, 256), vmem(8, 8, 256), vmem(8, 8, 256),
+            vmem(8, 8, 256), vmem(8, 8, 256), vmem(8, 8, 256),
             vmem(8, 8, 128), vmem(3, 8, 8, 128),
             pltpu.VMEM((256, 128), BF16), pltpu.VMEM((128, 256), BF16),
-            pltpu.SemaphoreType.DMA((10,)), pltpu.SemaphoreType.DMA((count,)), pltpu.SemaphoreType.DMA((count,)),
+            pltpu.SemaphoreType.REGULAR((4,)), pltpu.SemaphoreType.DMA((8,)), pltpu.SemaphoreType.DMA((count,)), pltpu.SemaphoreType.DMA((count,)),
         ],
         compiler_params=pltpu.CompilerParams(
             collective_id=0, has_side_effects=True, vmem_limit_bytes=32 * 1024 * 1024
         ),
     )(*[pltpu.with_memory_space_constraint(a, pltpu.HBM) for a in args])
+    return both[:8], both[8:]
 
 
 def solution(mesh):

time: 34.8 us -> 31.2 us (0.90)
  Pallas kernels: 32.8 us -> 29.7 us
  local copies, waits for them, and re-layouts: 1.31 us -> 0.72 us
    pallas_call x1, Pallas kernels: 32.8 us -> 29.7 us  [body(): pl.pallas_call(kernel, out_shape=pltpu.VMEM((16, 4096), F32), in_specs=[a...]
    unnamed x2 -> x0, local copies, waits for them, and re-layouts: 1.31 us -> none
    slice x0 -> x1, local copies, waits for them, and re-layouts: none -> 0.72 us  [body(): return (both[:8], both[8:])]
where the time goes in v2:
time: 31.2 us; the launch traced here: 31.1 us
  Pallas kernels  29.7 us (95%)
  local copies, waits for them, and re-layouts  0.72 us (2%)
  between operations  0.64 us (2%)
    pallas_call x1, Pallas kernels, body(): pl.pallas_call(kernel, out_shape=pltpu.VMEM((16, 4096), F32), in_specs=[a...  29.7 us
    slice x1, local copies, waits for them, and re-layouts, body(): return (both[:8], both[8:])  0.72 us

profile of v2, /device:TPU:1, one launch (start us, length us, event | category | flops | bytes accessed | tf_op | source)
XLA Modules:
  0.0 31.1 jit_solution(4588454056338242311)
XLA Ops:
  0.6 29.7 %shard_map.95 = f32[16,4096]{1,0:T(8,128)S(1)} custom-call(f32[8,4096]{1,0:T(8,128)} %init_h.1, f32[8,4096]{1,0:T(8,128)} %src_h.1, f32[8,4096]{1,0:T(8,128)} %perm_h.1, s32[8]{0:T(128)} %mx_h.1, s32[8]{0:T(128)} %my_h.1, s32[8,6]{1,0:T(8,128)} %nb_h.1, s32[8]{0:T(128)} %ch_h.1, s32[8]{0:T(128)} %pa_h.1), custom_call_target="tpu_custom_call" | custom-call | tf_op jit(solution)/shard_map/pallas_call | solution.py:564
  30.3 0.7 %fusion = (f32[8,4096]{1,0:T(8,128)}, f32[8,4096]{1,0:T(8,128)}) fusion(f32[16,4096]{1,0:T(8,128)S(1)} %shard_map.95), kind=kLoop, calls=%fused_computation | loop fusion | bytes 524288 | tf_op jit(solution)/shard_map/slice | solution.py:588

commit v3 on v2

--- a/solution.py
+++ b/solution.py
@@ -58,7 +58,7 @@
     init_h, src_h, perm_h, mx_h, my_h, nb_h, ch_h, pa_h, both_v,
     own, px, t_mx, t_my, t_ch, t_pa, nbv, msg_s, msg_r, yi_s, yi_r, yf_s, yf_r,
     vv, fr, qr, sb, sc, gb, gc, every_s, every_r, gs, gr, ps, pxr, pyr, pd_s, pd_r,
-    e0, ef, eq, cor, zz, restrict_m, upsample_m,
+    flux_v, squares_v, e0, ef, eq, cor, zz, restrict_m, upsample_m,
     ready, lsem, ssem, rsem,
 ):
     va, vb = vv.at[0], vv.at[1]
@@ -222,6 +222,9 @@
     here_b = jnp.where(left_half, away[2], away[3]) == 0
     row_c = jnp.where(left_c, slot[4], slot[5])
     here_c = jnp.where(left_c, away[4], away[5]) == 0
+    sent = [(d >= 1) & (d <= 4) for d in away]
+    sent_b = (low_b & sent[2], high_b & sent[3])
+    sent_c = (low_c & sent[4]) | (high_c & sent[5])
 
     def pack_faces(v):
         packed = [[v[1, :, 0:128], v[1, :, 128:256]], [v[16, :, 0:128], v[16, :, 128:256]]]
@@ -266,10 +269,10 @@
                 end[0, :, cols] = low
                 end[17, :, cols] = high
         for a in range(16):
-            gb[a] = rows(sb[a], row_b)
+            gb[a] = jnp.where(here_b, rows(sb[a], row_b), 0.0)
             for h in range(2):
                 cols = slice(128 * h, 128 * h + 128)
-                gc[a, :, cols] = rows(sc[a, :, cols], row_c)
+                gc[a, :, cols] = jnp.where(here_c, rows(sc[a, :, cols], row_c), 0.0)
 
     def take_faces(got, ends, copies):
         for copy in copies:
@@ -301,8 +304,8 @@
     def parts(before, x, after, ghost_b, ghost_c):
         down, up = [roll(y, 16) for y in x], [roll(y, -16) for y in x]
         beside_b = (
-            (jnp.where(low_b, ghost_b, down[0]), jnp.where(high_b, up[1], up[0])),
-            (jnp.where(low_b, down[0], down[1]), jnp.where(high_b, ghost_b, up[1])),
+            (jnp.where(low_b, ghost_b[0], down[0]), jnp.where(high_b, up[1], up[0])),
+            (jnp.where(low_b, down[0], down[1]), jnp.where(high_b, ghost_b[1], up[1])),
         )
         out = []
         for h in range(2):
@@ -323,12 +326,46 @@
     def stencil(v, a, ghost_b, ghost_c):
         return parts(halves(v, a), halves(v, a + 1), halves(v, a + 2), ghost_b, ghost_c)
 
-    def fine_ghosts(a):
-        return gb[a], (gc[a, :, 0:128], gc[a, :, 128:256])
-
-    def jacobi(v, force, coefficient, ghosts, store, count):
+    def whole(v, a):
+        return stencil(v, a, (gb[a], gb[a]), (gc[a, :, 0:128], gc[a, :, 128:256]))
+
+    def begin(v):
+        for a in range(16):
+            x = halves(v, a + 1)
+            ends = [halves(v, a), halves(v, a + 2)]
+            if a == 0:
+                ends[0] = [jnp.where(sent[0], x[h], ends[0][h]) for h in range(2)]
+            if a == 15:
+                ends[1] = [jnp.where(sent[1], x[h], ends[1][h]) for h in range(2)]
+            ghost_b = [jnp.where(sent_b[h], x[h], gb[a]) for h in range(2)]
+            ghost_c = [jnp.where(sent_c, x[h], gc[a, :, 128 * h : 128 * h + 128]) for h in range(2)]
+            for h, (_, flux, squares) in enumerate(parts(ends[0], x, ends[1], ghost_b, ghost_c)):
+                flux_v[a, :, 128 * h : 128 * h + 128] = flux
+                squares_v[a, :, 128 * h : 128 * h + 128] = squares
+
+    def complete(v, a):
+        out = []
+        for h, x in enumerate(halves(v, a + 1)):
+            cols = slice(128 * h, 128 * h + 128)
+            ghosts = [(sent_b[h], gb[a]), (sent_c, gc[a, :, cols])]
+            if a == 0:
+                ghosts.append((sent[0], v[0, :, cols]))
+            if a == 15:
+                ghosts.append((sent[1], v[17, :, cols]))
+            own_square = x * x
+            mobility = 1.0 + own_square
+            flux, squares = flux_v[a, :, cols], squares_v[a, :, cols]
+            for mask, ghost in ghosts:
+                w = jnp.where(mask, ghost, x)
+                square = w * w
+                flux = flux + (mobility + square) * (x - w)
+                squares = squares + (square - own_square)
+            out.append((x, flux, squares))
+        return out
+
+    def jacobi(v, force, coefficient, sums, store, count):
         for a in range(count):
-            for h, (x, flux, conduct) in enumerate(stencil(v, a, *ghosts(a))):
+            for h, (x, flux, conduct) in enumerate(sums(v, a)):
                 cols = slice(128 * h, 128 * h + 128)
                 q = coefficient[a, :, cols]
                 defect = force[a, :, cols] - (REACTION * x + q * flux)
@@ -342,7 +379,7 @@
 
     def smooth(sweeps):
         for n in range(sweeps):
-            jacobi(vv.at[n % 2], fr, qr, fine_ghosts, into(vv.at[(n + 1) % 2]), 16)
+            jacobi(vv.at[n % 2], fr, qr, whole if n else complete, into(vv.at[(n + 1) % 2]), 16)
 
     def shrink(n, layer):
         fold = jnp.concatenate([layer(2 * a) + layer(2 * a + 1) for a in range(8)], 0)
@@ -385,6 +422,7 @@
     for copy in copies0:
         copy.start()
     own_faces(va, (va, vb))
+    begin(va)
 
     marks = jnp.concatenate([(lane == d).astype(F32) for d in away], 0)
     before = (
@@ -441,13 +479,14 @@
 
     copies1 = send_faces(1, vb)
     own_faces(vb, (vb,))
+    begin(vb)
     sol_copies = shrink(0, lambda a: vb[a + 1])
     take_faces(asked(1), (vb,), copies1)
 
     layers = []
     for a in range(16):
         layers.append([])
-        for h, (x, flux, _) in enumerate(stencil(vb, a, *fine_ghosts(a))):
+        for h, (x, flux, _) in enumerate(complete(vb, a)):
             cols = slice(128 * h, 128 * h + 128)
             value = fr[a, :, cols] - (REACTION * x + qr[a, :, cols] * flux)
             both_v[8:16, 256 * a + 128 * h : 256 * a + 128 * h + 128] = value
@@ -497,28 +536,32 @@
     def store_0(a, t, value):
         coarse[a][t] = value
 
-    def store_f(a, t, value):
-        cols = slice(128 * t, 128 * t + 128)
-        ef[a, :, cols] = ef[a, :, cols] + value
-
     def coarse_parts(e):
         other = sub + 1 - 2 * half_a
         below = [jnp.where(half_a == 1, rows(e[7][t], other), 0.0) for t in range(2)]
         above = [jnp.where(half_a == 0, rows(e[0][t], other), 0.0) for t in range(2)]
         layers = [below] + e + [above]
-        return [parts(*layers[a : a + 3], zero, (zero, zero)) for a in range(8)]
+        return [parts(*layers[a : a + 3], (zero, zero), (zero, zero)) for a in range(8)]
 
     assemble(2, perm_copies, store_q)
     assemble(0, sol_copies, store_0)
+    iterate = [[None, None] for _ in range(8)]
+    pace = [[None, None] for _ in range(8)]
     for a, part in enumerate(coarse_parts(coarse)):
-        for h, (x, flux, _) in enumerate(part):
+        for h, (x, flux, conduct) in enumerate(part):
             cols = slice(128 * h, 128 * h + 128)
             e0[a, :, cols] = x
             ef[a, :, cols] = REACTION * x + eq[a, :, cols] * flux
+            pace[a][h] = DAMPING / (REACTION + eq[a, :, cols] * conduct)
+
+    def store_f(a, t, value):
+        cols = slice(128 * t, 128 * t + 128)
+        ef[a, :, cols] = ef[a, :, cols] + value
+        iterate[a][t] = coarse[a][t] + value * pace[a][t]
+
     assemble(1, res_copies, store_f)
 
-    iterate = coarse
-    for repeat in range(COARSE):
+    for repeat in range(COARSE - 1):
         after = []
         for a, part in enumerate(coarse_parts(iterate)):
             after.append([])
@@ -543,13 +586,14 @@
 
     copies2 = send_faces(2, va)
     own_faces(va, (va, vb))
+    begin(va)
     take_faces(asked(2), (va, vb), copies2)
 
     def into_result(a, h, value):
         both_v[0:8, 256 * a + 128 * h : 256 * a + 128 * h + 128] = value
 
     smooth(INNER - 1)
-    jacobi(va, fr, qr, fine_ghosts, into_result, 16)
+    jacobi(va, fr, qr, whole, into_result, 16)
 
     for copy in (
         x_copies + msgs + [y_first, y_second] + copies0 + perm_copies + copies1 + sol_copies + res_copies + copies2
@@ -576,7 +620,7 @@
             vmem(6, 8, 256), vmem(4, 6, 8, 256), vmem(2, 4, 8, 256), vmem(2, 4, 8, 256),
             vmem(3, 4, 8, 128), vmem(3, 4, 8, 128), vmem(3, 4, 8, 128),
             vmem(3, 4, 2, 128), vmem(3, 4, 2, 128),
-            vmem(8, 8, 256), vmem(8, 8, 256), vmem(8, 8, 256),
+            vmem(16, 8, 256), vmem(16, 8, 256), vmem(8, 8, 256), vmem(8, 8, 256), vmem(8, 8, 256),
             vmem(8, 8, 128), vmem(3, 8, 8, 128),
             pltpu.VMEM((256, 128), BF16), pltpu.VMEM((128, 256), BF16),
             pltpu.SemaphoreType.REGULAR((4,)), pltpu.SemaphoreType.DMA((8,)), pltpu.SemaphoreType.DMA((count,)), pltpu.SemaphoreType.DMA((count,)),

time: 31.2 us -> 30.7 us (0.984)
  Pallas kernels: 29.7 us -> 29.3 us
    pallas_call x1, Pallas kernels: 29.7 us -> 29.3 us  [body(): pl.pallas_call(kernel, out_shape=pltpu.VMEM((16, 4096), F32), in_specs=[a...]
where the time goes in v3:
time: 30.7 us; the launch traced here: 30.6 us
  Pallas kernels  29.3 us (95%)
  local copies, waits for them, and re-layouts  0.72 us (2%)
  between operations  0.64 us (2%)
    pallas_call x1, Pallas kernels, body(): pl.pallas_call(kernel, out_shape=pltpu.VMEM((16, 4096), F32), in_specs=[a...  29.3 us
    slice x1, local copies, waits for them, and re-layouts, body(): return (both[:8], both[8:])  0.72 us

profile of v3, /device:TPU:1, one launch (start us, length us, event | category | flops | bytes accessed | tf_op | source)
XLA Modules:
  0.0 30.6 jit_solution(11013897644882050906)
XLA Ops:
  0.6 29.3 %shard_map.95 = f32[16,4096]{1,0:T(8,128)S(1)} custom-call(f32[8,4096]{1,0:T(8,128)} %init_h.1, f32[8,4096]{1,0:T(8,128)} %src_h.1, f32[8,4096]{1,0:T(8,128)} %perm_h.1, s32[8]{0:T(128)} %mx_h.1, s32[8]{0:T(128)} %my_h.1, s32[8,6]{1,0:T(8,128)} %nb_h.1, s32[8]{0:T(128)} %ch_h.1, s32[8]{0:T(128)} %pa_h.1), custom_call_target="tpu_custom_call" | custom-call | tf_op jit(solution)/shard_map/pallas_call | solution.py:608
  29.9 0.7 %fusion = (f32[8,4096]{1,0:T(8,128)}, f32[8,4096]{1,0:T(8,128)}) fusion(f32[16,4096]{1,0:T(8,128)S(1)} %shard_map.95), kind=kLoop, calls=%fused_computation | loop fusion | bytes 524288 | tf_op jit(solution)/shard_map/slice | solution.py:632

commit v4 on v3

--- a/solution.py
+++ b/solution.py
@@ -86,8 +86,8 @@
     for copy in fields:
         copy.start()
 
-    even = (i + j) % 2 == 0
-    odd = (i + j) % 2 == 1
+    even = (i + j) % 2 == 1
+    odd = (i + j) % 2 == 0
     barrier = pltpu.get_barrier_semaphore()
 
     def signal(semaphore, peer):
@@ -136,7 +136,8 @@
             for d in range(4)
         ]
 
-    x_copies = [push(a, px.at[n], xp) for n, a in enumerate((init_h, src_h, perm_h))]
+    fields[0].wait()
+    x_copies = [push(a, px.at[n], xp) for n, a in enumerate((own.at[0], src_h, perm_h))]
     for copy in x_copies:
         copy.start()
 
@@ -181,7 +182,6 @@
         cols = pl.ds(128 * c, 128)
         return jnp.where(leave_own, rows(own[n, :, cols], leave_row), rows(px[n, :, cols], leave_row))
 
-    fields[0].wait()
     x_copies[0].wait_recv()
     for c in range(32):
         yi_s[c] = leaving(0, c)[0:2]

time: 30.7 us -> 30.4 us (level)
  Pallas kernels: 29.3 us -> 28.9 us
    pallas_call x1, Pallas kernels: 29.3 us -> 28.9 us  [body(): pl.pallas_call(kernel, out_shape=pltpu.VMEM((16, 4096), F32), in_specs=[a...]
where the time goes in v4:
time: 30.4 us; the launch traced here: 30.3 us
  Pallas kernels  28.9 us (95%)
  local copies, waits for them, and re-layouts  0.72 us (2%)
  between operations  0.64 us (2%)
    pallas_call x1, Pallas kernels, body(): pl.pallas_call(kernel, out_shape=pltpu.VMEM((16, 4096), F32), in_specs=[a...  28.9 us
    slice x1, local copies, waits for them, and re-layouts, body(): return (both[:8], both[8:])  0.72 us

profile of v4, /device:TPU:1, one launch (start us, length us, event | category | flops | bytes accessed | tf_op | source)
XLA Modules:
  0.0 30.3 jit_solution(16037679515584759009)
XLA Ops:
  0.6 28.9 %shard_map.95 = f32[16,4096]{1,0:T(8,128)S(1)} custom-call(f32[8,4096]{1,0:T(8,128)} %init_h.1, f32[8,4096]{1,0:T(8,128)} %src_h.1, f32[8,4096]{1,0:T(8,128)} %perm_h.1, s32[8]{0:T(128)} %mx_h.1, s32[8]{0:T(128)} %my_h.1, s32[8,6]{1,0:T(8,128)} %nb_h.1, s32[8]{0:T(128)} %ch_h.1, s32[8]{0:T(128)} %pa_h.1), custom_call_target="tpu_custom_call" | custom-call | tf_op jit(solution)/shard_map/pallas_call | solution.py:608
  29.6 0.7 %fusion = (f32[8,4096]{1,0:T(8,128)}, f32[8,4096]{1,0:T(8,128)}) fusion(f32[16,4096]{1,0:T(8,128)S(1)} %shard_map.95), kind=kLoop, calls=%fused_computation | loop fusion | bytes 524288 | tf_op jit(solution)/shard_map/slice | solution.py:632

commit v5 on v4

--- a/solution.py
+++ b/solution.py
@@ -137,9 +137,11 @@
         ]
 
     fields[0].wait()
-    x_copies = [push(a, px.at[n], xp) for n, a in enumerate((own.at[0], src_h, perm_h))]
-    for copy in x_copies:
-        copy.start()
+    x_copies = [push(own.at[0], px.at[0], xp), push(own.at[1:3], px.at[1:3], xp)]
+    x_copies[0].start()
+    fields[1].wait()
+    fields[2].wait()
+    x_copies[1].start()
 
     lane = lax.broadcasted_iota(I32, (8, 128), 1)
     sub = lax.broadcasted_iota(I32, (8, 128), 0)
@@ -199,9 +201,7 @@
         signal(ready.at[2], beyond_x)
         signal(ready.at[3], beyond_y)
 
-    for n in (1, 2):
-        fields[n].wait()
-        x_copies[n].wait_recv()
+    x_copies[1].wait_recv()
     for c in range(32):
         yf_s[c] = jnp.where(sub < 2, leaving(1, c), leaving(2, c))[0:4]
     y_second = push(yf_s, yf_r, yp)
@@ -390,10 +390,12 @@
             dense = jnp.where(left_c, out[16 * m : 16 * m + 8], out[16 * m + 8 : 16 * m + 16])
             ps[n, m] = dense
             pd_s[n, m] = rows(dense, outward)[0:2]
+
+    def send_pieces(which):
         copies = [
-            push(ps.at[n], pxr.at[n], xp),
-            push(ps.at[n], pyr.at[n], yp),
-            push(pd_s.at[n], pd_r.at[n], diag),
+            push(ps.at[which], pxr.at[which], xp),
+            push(ps.at[which], pyr.at[which], yp),
+            push(pd_s.at[which], pd_r.at[which], diag),
         ]
         for copy in copies:
             copy.start()
@@ -460,7 +462,7 @@
         cols = slice(128 * (c % 2), 128 * (c % 2) + 128)
         fr[c // 2, :, cols] = arrived(1, yf_r, 0, c)
         qr[c // 2, :, cols] = 0.5 * arrived(2, yf_r, 2, c)
-    perm_copies = shrink(2, lambda a: qr[a])
+    shrink(0, lambda a: qr[a])
     take_faces(lambda d, f, cols: rows(every_r[d, f ^ 1, :, cols], slot[f]), (va, vb), copies0)
     smooth(INNER)
 
@@ -480,7 +482,8 @@
     copies1 = send_faces(1, vb)
     own_faces(vb, (vb,))
     begin(vb)
-    sol_copies = shrink(0, lambda a: vb[a + 1])
+    shrink(1, lambda a: vb[a + 1])
+    sol_copies = send_pieces(pl.ds(0, 2))
     take_faces(asked(1), (vb,), copies1)
 
     layers = []
@@ -491,7 +494,8 @@
             value = fr[a, :, cols] - (REACTION * x + qr[a, :, cols] * flux)
             both_v[8:16, 256 * a + 128 * h : 256 * a + 128 * h + 128] = value
             layers[a].append(value)
-    res_copies = shrink(1, lambda a: jnp.concatenate(layers[a], 1))
+    shrink(2, lambda a: jnp.concatenate(layers[a], 1))
+    res_copies = send_pieces(2)
 
     block, half_a = sub // 2, sub % 2
     side_c = (lane // 8) % 2
@@ -543,8 +547,8 @@
         layers = [below] + e + [above]
         return [parts(*layers[a : a + 3], (zero, zero), (zero, zero)) for a in range(8)]
 
-    assemble(2, perm_copies, store_q)
-    assemble(0, sol_copies, store_0)
+    assemble(0, sol_copies, store_q)
+    assemble(1, [], store_0)
     iterate = [[None, None] for _ in range(8)]
     pace = [[None, None] for _ in range(8)]
     for a, part in enumerate(coarse_parts(coarse)):
@@ -559,7 +563,7 @@
         ef[a, :, cols] = ef[a, :, cols] + value
         iterate[a][t] = coarse[a][t] + value * pace[a][t]
 
-    assemble(1, res_copies, store_f)
+    assemble(2, res_copies, store_f)
 
     for repeat in range(COARSE - 1):
         after = []
@@ -596,7 +600,7 @@
     jacobi(va, fr, qr, whole, into_result, 16)
 
     for copy in (
-        x_copies + msgs + [y_first, y_second] + copies0 + perm_copies + copies1 + sol_copies + res_copies + copies2
+        x_copies + msgs + [y_first, y_second] + copies0 + copies1 + sol_copies + res_copies + copies2
     ):
         copy.wait_send()
 

time: 30.4 us -> 30.3 us (level)
  no operation moved by 1% of the time
where the time goes in v5:
time: 30.3 us; the launch traced here: 30.2 us
  Pallas kernels  28.8 us (95%)
  local copies, waits for them, and re-layouts  0.72 us (2%)
  between operations  0.64 us (2%)
    pallas_call x1, Pallas kernels, body(): pl.pallas_call(kernel, out_shape=pltpu.VMEM((16, 4096), F32), in_specs=[a...  28.8 us
    slice x1, local copies, waits for them, and re-layouts, body(): return (both[:8], both[8:])  0.72 us

profile of v5, /device:TPU:1, one launch (start us, length us, event | category | flops | bytes accessed | tf_op | source)
XLA Modules:
  0.0 30.2 jit_solution(18187882988437447128)
XLA Ops:
  0.6 28.8 %shard_map.95 = f32[16,4096]{1,0:T(8,128)S(1)} custom-call(f32[8,4096]{1,0:T(8,128)} %init_h.1, f32[8,4096]{1,0:T(8,128)} %src_h.1, f32[8,4096]{1,0:T(8,128)} %perm_h.1, s32[8]{0:T(128)} %mx_h.1, s32[8]{0:T(128)} %my_h.1, s32[8,6]{1,0:T(8,128)} %nb_h.1, s32[8]{0:T(128)} %ch_h.1, s32[8]{0:T(128)} %pa_h.1), custom_call_target="tpu_custom_call" | custom-call | tf_op jit(solution)/shard_map/pallas_call | solution.py:612
  29.5 0.7 %fusion = (f32[8,4096]{1,0:T(8,128)}, f32[8,4096]{1,0:T(8,128)}) fusion(f32[16,4096]{1,0:T(8,128)S(1)} %shard_map.95), kind=kLoop, calls=%fused_computation | loop fusion | bytes 524288 | tf_op jit(solution)/shard_map/slice | solution.py:636

commit v6 on v5

--- a/solution.py
+++ b/solution.py
@@ -301,7 +301,7 @@
     def halves(v, a):
         return [v[a, :, 0:128], v[a, :, 128:256]]
 
-    def parts(before, x, after, ghost_b, ghost_c):
+    def parts(before, x, after, ghost_b, ghost_c, shared=None):
         down, up = [roll(y, 16) for y in x], [roll(y, -16) for y in x]
         beside_b = (
             (jnp.where(low_b, ghost_b[0], down[0]), jnp.where(high_b, up[1], up[0])),
@@ -315,19 +315,29 @@
                 before[h],
                 after[h],
             )
-            mobility = 1.0 + x[h] * x[h]
-            square = [w * w for w in beside]
-            term = [(mobility + y) * (x[h] - w) for y, w in zip(square, beside)]
+            last = shared.get(h) if shared is not None else None
+            own_square = last[1] if last else x[h] * x[h]
+            mobility = 1.0 + own_square
+            square = [w * w for w in beside[:4]] + [last[2] if last else before[h] * before[h], after[h] * after[h]]
+            term = [(mobility + y) * (x[h] - w) for y, w in zip(square[:4], beside)]
+            above = (mobility + square[5]) * (x[h] - after[h])
+            ends = above - last[0] if last else above + (mobility + square[4]) * (x[h] - before[h])
+            if shared is not None:
+                shared[h] = (above, square[5], own_square)
             squares = 6.0 * mobility + pairwise(square)
-            flux = pairwise(term)
+            flux = ((term[0] + term[1]) + (term[2] + term[3])) + ends
             out.append((x[h], flux, squares))
         return out
 
-    def stencil(v, a, ghost_b, ghost_c):
-        return parts(halves(v, a), halves(v, a + 1), halves(v, a + 2), ghost_b, ghost_c)
+    def stencil(v, a, ghost_b, ghost_c, shared):
+        return parts(halves(v, a), halves(v, a + 1), halves(v, a + 2), ghost_b, ghost_c, shared)
+
+    edges = {}
 
     def whole(v, a):
-        return stencil(v, a, (gb[a], gb[a]), (gc[a, :, 0:128], gc[a, :, 128:256]))
+        if a == 0:
+            edges.clear()
+        return stencil(v, a, (gb[a], gb[a]), (gc[a, :, 0:128], gc[a, :, 128:256]), edges)
 
     def begin(v):
         for a in range(16):
@@ -545,7 +555,8 @@
         below = [jnp.where(half_a == 1, rows(e[7][t], other), 0.0) for t in range(2)]
         above = [jnp.where(half_a == 0, rows(e[0][t], other), 0.0) for t in range(2)]
         layers = [below] + e + [above]
-        return [parts(*layers[a : a + 3], (zero, zero), (zero, zero)) for a in range(8)]
+        shared = {}
+        return [parts(*layers[a : a + 3], (zero, zero), (zero, zero), shared) for a in range(8)]
 
     assemble(0, sol_copies, store_q)
     assemble(1, [], store_0)

time: 30.3 us -> 30.2 us (level)
  no operation moved by 1% of the time
where the time goes in v6:
time: 30.2 us; the launch traced here: 30.1 us
  Pallas kernels  28.7 us (95%)
  local copies, waits for them, and re-layouts  0.72 us (2%)
  between operations  0.64 us (2%)
    pallas_call x1, Pallas kernels, body(): pl.pallas_call(kernel, out_shape=pltpu.VMEM((16, 4096), F32), in_specs=[a...  28.7 us
    slice x1, local copies, waits for them, and re-layouts, body(): return (both[:8], both[8:])  0.72 us

profile of v6, /device:TPU:1, one launch (start us, length us, event | category | flops | bytes accessed | tf_op | source)
XLA Modules:
  0.0 30.1 jit_solution(13270659803214635567)
XLA Ops:
  0.6 28.7 %shard_map.95 = f32[16,4096]{1,0:T(8,128)S(1)} custom-call(f32[8,4096]{1,0:T(8,128)} %init_h.1, f32[8,4096]{1,0:T(8,128)} %src_h.1, f32[8,4096]{1,0:T(8,128)} %perm_h.1, s32[8]{0:T(128)} %mx_h.1, s32[8]{0:T(128)} %my_h.1, s32[8,6]{1,0:T(8,128)} %nb_h.1, s32[8]{0:T(128)} %ch_h.1, s32[8]{0:T(128)} %pa_h.1), custom_call_target="tpu_custom_call" | custom-call | tf_op jit(solution)/shard_map/pallas_call | solution.py:623
  29.4 0.7 %fusion = (f32[8,4096]{1,0:T(8,128)}, f32[8,4096]{1,0:T(8,128)}) fusion(f32[16,4096]{1,0:T(8,128)S(1)} %shard_map.95), kind=kLoop, calls=%fused_computation | loop fusion | bytes 524288 | tf_op jit(solution)/shard_map/slice | solution.py:647
